TPU v7x, 256 devices: a whole 4x4x8 slice. The times are simulated.
256 devices in a mesh: gx: 8 (over x, core), gy: 32 (over z, y).
Axes of the slice: x: 4, y: 4, z: 8, core: 2. Of those that a mesh axis runs over, the one named last changes fastest.
Arguments:
- right_side: float32 [256, 1024, 128], P('gx', 'gy'), may hold values from -38 to 38
- guess: float32 [256, 1024, 128], P('gx', 'gy'), may hold values from -3 to 3
- conductivity: float32 [256, 1024, 128], P('gx', 'gy'), may hold values from 0.5 to 4
- wet_mask: int32 [256, 1024, 128], P('gx', 'gy'), may hold values from 0 to 1, as said below
- coarse_map: int32 [16, 64, 1], P('gx', 'gy'), may hold values from 0 to 1023
- coarse_inverse: float32 [1024, 1024], P(('gx', 'gy')), may hold values from -6.473756e-05 to 0.0028268734
Outputs:
- pressure: float32 [256, 1024, 128], P('gx', 'gy')
- residual: float32 [256, 1024, 128], P('gx', 'gy')
Inputs may be any that keep to these rules, and one draw needn't show every extreme that they name: `wet_mask`: 1 marks a wet cell and 0 a dry one; the dry cells of each column of levels are its lowest ones. `coarse_map`: every coarse node 0 to 1023 is named by at least one block.
All inputs are finite; a program needn't handle non-finite values.
Results may differ from a plain program's by a relative error of at most 0.0003.
Values sent between devices are 32-bit elements; how exact they have to be, the bound alone decides.
A program may use at most 64 MiB of HBM per device.

v0:
```python
import jax
import jax.numpy as jnp
from jax import lax
from jax.sharding import PartitionSpec as P

BLK = 16
MARGIN = 2
SWEEPS = 4


screen = 0.02
relax = 0.8


def with_halo(array, sides, width):
    for axis, dim in sides:
        size, length = (lax.axis_size(axis), array.shape[dim])
        up = [(i, (i + 1) % size) for i in range(size - 1)]
        down = [(j, i) for i, j in up]
        last = lax.slice_in_dim(array, length - width, length, axis=dim)
        initial = lax.slice_in_dim(array, 0, width, axis=dim)
        before = lax.ppermute(last, axis, up)
        after = lax.ppermute(initial, axis, down)
        array = jnp.concatenate([before, array, after], axis=dim)
    return array


def face_weights(cond):
    zpad = jnp.pad(cond, ((0, 0), (0, 0), (1, 1)))
    center = cond[1:-1, 1:-1, :]
    west = jnp.minimum(center, cond[:-2, 1:-1, :])
    east = jnp.minimum(center, cond[2:, 1:-1, :])
    south = jnp.minimum(center, cond[1:-1, :-2, :])
    north = jnp.minimum(center, cond[1:-1, 2:, :])
    below = jnp.minimum(center, zpad[1:-1, 1:-1, :-2])
    above = jnp.minimum(center, zpad[1:-1, 1:-1, 2:])
    diag = (
        screen + jnp.maximum(0.0, 1.0 - 2.0 * center) + west + east + south + north + below + above
    )
    return (diag, (west, east, south, north, below, above))


def neighbours(field, weights):
    west, east, south, north, below, above = weights
    zpad = jnp.pad(field, ((0, 0), (0, 0), (1, 1)))
    total = west * field[:-2, 1:-1] + east * field[2:, 1:-1]
    total = total + south * field[1:-1, :-2] + north * field[1:-1, 2:]
    return total + below * zpad[1:-1, 1:-1, :-2] + above * zpad[1:-1, 1:-1, 2:]


def operate(field, diag, weights):
    return diag * field[1:-1, 1:-1] - neighbours(field, weights)


def smooth(resid, diag, weights):
    correction = relax * resid / diag
    for sweep in range(SWEEPS - 1):
        padded = jnp.pad(correction, ((1, 1), (1, 1), (0, 0)))
        correction = (
            correction + relax * (resid - diag * correction + neighbours(padded, weights)) / diag
        )
    return correction


def body(right_side, guess, conductivity, wet_mask, coarse_map, coarse_inverse):
    size_x, size_y, levels = right_side.shape
    cond = conductivity * wet_mask.astype(jnp.float32)
    wide = MARGIN + 1
    stacked = jnp.stack([cond, guess])
    padded = with_halo(stacked, (("gx", 1), ("gy", 2)), wide)
    diag_ext, weights_ext = face_weights(padded[0])
    diag = diag_ext[MARGIN : MARGIN + size_x, MARGIN : MARGIN + size_y]
    weights = tuple(
        (part[MARGIN : MARGIN + size_x, MARGIN : MARGIN + size_y] for part in weights_ext)
    )
    guess_near = padded[1][MARGIN : MARGIN + size_x + 2, MARGIN : MARGIN + size_y + 2]
    resid = right_side - operate(guess_near, diag, weights)
    resid_ext = with_halo(resid, (("gx", 0), ("gy", 1)), MARGIN)
    blocks_x = size_x // BLK
    blocks_y = size_y // BLK
    block_sums = resid.reshape(blocks_x, BLK, blocks_y, BLK, levels).sum(axis=(1, 3, 4)).reshape(-1)
    nodes = coarse_map.reshape(-1)
    total_nodes = coarse_inverse.shape[1]
    onehot = (nodes[:, None] == jnp.arange(total_nodes, dtype=jnp.int32)[None, :]).astype(
        jnp.float32
    )
    partial_resid = jnp.dot(block_sums, onehot, precision=lax.Precision.HIGHEST)
    coarse_resid = lax.psum(partial_resid, ("gx", "gy"))
    local = smooth(resid_ext, diag_ext, weights_ext)[
        MARGIN : MARGIN + size_x, MARGIN : MARGIN + size_y
    ]
    own_corr = jnp.dot(coarse_inverse, coarse_resid, precision=lax.Precision.HIGHEST)
    coarse_corr = lax.all_gather(own_corr, ("gx", "gy"), axis=0, tiled=True)
    block_corr = jnp.dot(onehot, coarse_corr, precision=lax.Precision.HIGHEST).reshape(
        blocks_x, blocks_y
    )
    direction = (
        local.reshape(blocks_x, BLK, blocks_y, BLK, levels) + block_corr[:, None, :, None, None]
    ).reshape(size_x, size_y, levels)
    direction_near = with_halo(direction, (("gx", 0), ("gy", 1)), 1)
    image = operate(direction_near, diag, weights)
    numer, denom = lax.psum((jnp.sum(resid * direction), jnp.sum(direction * image)), ("gx", "gy"))
    alpha = numer / denom
    return (guess + alpha * direction, resid - alpha * image)


def solution(mesh):
    in_specs = (
        P("gx", "gy", None),
        P("gx", "gy", None),
        P("gx", "gy", None),
        P("gx", "gy", None),
        P("gx", "gy", None),
        P(("gx", "gy"), None),
    )
    out_specs = (P("gx", "gy", None), P("gx", "gy", None))
    return jax.shard_map(body, mesh=mesh, in_specs=in_specs, out_specs=out_specs, check_vma=False)
```

profile of v0, /device:TPU:1, one launch (start us, length us, event | category | flops | bytes accessed | tf_op | source)
XLA Modules:
  0.0 316.7 jit_solution(4383092690689171364)
XLA Ops:
  0.6 0.0 copy-start
  0.6 0.0 copy-start.8
  0.7 1.3 multiply_bitcast_fusion
  2.0 0.0 copy-start.11
  2.1 5.1 %collective-permute-start.1 = (f32[2,3,32,128]{3,2,1,0:T(8,128)S(1)}, f32[2,3,32,128]{3,2,1,0:T(8,128)S(1)}, u32[]{:S(2)}, u32[]{:S(2)}) collective-permute-start(f32[2,3,32,128]{3,2,1,0:T(8,128)S(1)} %get-tuple-element.21), channel_id=1, source_target_pairs={{32,0},{64,32},{96,64},{128,96},{160,128},{192,160},{224,192},{33,... | collective-permute-start | bytes 294920 | tf_op jit(solution)/shard_map/ppermute | solution.py:23
  7.2 1.9 collective-permute-start
  9.1 1.6 collective-permute-done
  10.8 0.1 pad_maximum_fusion.13
  10.8 1.3 collective-permute-start.3
  12.1 4.0 %collective-permute-start.2 = (f32[2,38,3,128]{3,2,1,0:T(4,128)S(1)}, f32[2,38,3,128]{3,2,1,0:T(4,128)S(1)}, u32[]{:S(2)}, u32[]{:S(2)}) collective-permute-start(f32[2,38,3,128]{3,2,1,0:T(4,128)S(1)} %get-tuple-element.18), channel_id=1, source_target_pairs={{0,1},{1,2},{2,3},{3,4},{4,5},{5,6},{6,7},{7,8},{8,9},{9,10},{10,1... | collective-permute-start | bytes 350216 | tf_op jit(solution)/shard_map/ppermute | solution.py:22
  16.1 0.5 broadcast.53
  16.7 0.7 reduce.5
  17.3 0.7 eq.15
  18.0 0.5 collective-permute-done.3
  18.5 1.0 collective-permute-done.2
  19.5 0.2 pad_maximum_fusion
  19.7 0.1 slice_bitcast_fusion
  19.8 0.6 add_add_fusion
  20.5 0.0 copy-start.9
  20.5 0.1 slice.271
  20.6 1.4 copy-done.9
  21.9 1.6 fusion.49
  23.6 0.6 fusion.54
  24.2 2.8 collective-permute-start.5
  27.0 3.4 %collective-permute-start.4 = (f32[2,32,128]{2,1,0:T(8,128)}, f32[2,32,128]{2,1,0:T(8,128)S(1)}, u32[]{:S(2)}, u32[]{:S(2)}) collective-permute-start(f32[2,32,128]{2,1,0:T(8,128)} %get-tuple-element.32), channel_id=1, source_target_pairs={{0,32},{32,64},{64,96},{96,128},{128,160},{160,192},{192,224},{1,3... | collective-permute-start | bytes 98312 | tf_op jit(solution)/shard_map/ppermute | solution.py:22
  30.4 1.4 reduce_sum.35
  31.8 1.5 reduce_sum.36
  33.2 1.3 reshape.17
  34.5 1.5 fusion.45
  36.0 83.7 %psum.21 = f32[1024]{0:T(1024)} all-reduce(f32[1024]{0:T(1024)} %bitcast.23), channel_id=1, replica_groups=mesh['gx'=8,'gy'=32] {'gx','gy'}, use_global_device_ids=true, to_apply=%region_2.3 | all-reduce | flops 1024 | bytes 8192 | tf_op jit(solution)/shard_map/psum | solution.py:88
  119.7 1.4 convolution_bitcast_fusion.1
  121.1 0.6 broadcast.24
  121.7 1.3 dynamic-update-slice
  123.0 72.7 %all-reduce.9 = f32[1024]{0:T(1024)} all-reduce(f32[1024]{0:T(1024)} %dynamic-update-slice), channel_id=1, replica_groups=mesh['gx'=8,'gy'=32] {'gx','gy'}, use_global_device_ids=true, to_apply=%add.9 | all-reduce | flops 1024 | bytes 8192
  195.8 0.7 pad_maximum_fusion.18
  196.4 1.3 collective-permute-start.7
  197.7 4.6 %collective-permute-start.6 = (f32[36,2,128]{2,1,0:T(2,128)}, f32[36,2,128]{2,1,0:T(2,128)}, u32[]{:S(2)}, u32[]{:S(2)}) collective-permute-start(f32[36,2,128]{2,1,0:T(2,128)} %get-tuple-element.26), channel_id=1, source_target_pairs={{0,1},{1,2},{2,3},{3,4},{4,5},{5,6},{6,7},{7,8},{8,9},{9,10},{10,1... | collective-permute-start | bytes 110600 | tf_op jit(solution)/shard_map/ppermute | solution.py:22
  202.3 1.4 convolution_bitcast_fusion
  203.7 1.2 add.193
  205.0 1.4 add.194
  206.3 1.4 add.195
  207.8 1.0 multiply_divide_fusion
  208.8 0.1 pad.32
  208.9 0.0 copy-done.6
  208.9 1.0 copy-done.2
  209.9 0.2 copy-done.4
  210.2 1.7 fusion.9
  211.9 0.1 pad.34
  211.9 1.7 fusion.17
  213.6 0.1 pad.36
  213.7 0.4 multiply_add_fusion
  214.1 0.4 fusion.19
  214.5 0.3 copy-done.10
  214.8 0.5 fusion.40
  215.4 3.1 collective-permute-start.9
  218.5 2.4 collective-permute-start.8
  220.9 0.8 collective-permute-done.8
  221.8 1.3 collective-permute-start.11
  223.1 4.0 %collective-permute-start.10 = (f32[34,1,128]{2,1,0:T(1,128)S(1)}, f32[34,1,128]{2,1,0:T(1,128)S(1)}, u32[]{:S(2)}, u32[]{:S(2)}) collective-permute-start(f32[34,1,128]{2,1,0:T(1,128)S(1)} %get-tuple-element.28), channel_id=1, source_target_pairs={{0,1},{1,2},{2,3},{3,4},{4,5},{5,6},{6,7},{7,8},{8,9},{9,10},{10,1... | collective-permute-start | bytes 52232 | tf_op jit(solution)/shard_map/ppermute | solution.py:22
  227.1 0.8 collective-permute-done.10
  228.0 0.6 select_maximum_fusion
  228.6 2.4 multiply_reduce_fusion
  231.0 81.9 %all-reduce.10 = (f32[]{:T(128)}, f32[]{:T(128)}) all-reduce(f32[]{:T(128)} %get-tuple-element.3, f32[]{:T(128)} %get-tuple-element.2), channel_id=1, replica_groups=mesh['gx'=8,'gy'=32] {'gx','gy'}, use_global_device_ids=true, to_apply=%region_4.5 | all-reduce | flops 2 | bytes 16 | tf_op jit(solution)/shard_map/psum | solution.py:102
  314.1 2.6 multiply_subtract_fusion
  (25 shorter events, 0.1 us)
Async XLA Ops:
  0.6 119.0 %copy-start = (f32[4,1024]{1,0:T(4,128)S(1)}, f32[4,1024]{1,0:T(4,128)}, u32[]{:S(2)}) copy-start(f32[4,1024]{1,0:T(4,128)} %param.11) | copy-start | bytes 49156
  0.6 1.4 copy-start.8
  2.0 14.6 %copy-start.11 = (s32[2,2,1]{1,2,0:T(1,128)S(1)}, s32[2,2,1]{1,2,0:T(1,128)}, u32[]{:S(2)}) copy-start(s32[2,2,1]{1,2,0:T(1,128)} %param.10) | copy-start | bytes 52
  2.1 7.1 %collective-permute-start.1 = (f32[2,3,32,128]{3,2,1,0:T(8,128)S(1)}, f32[2,3,32,128]{3,2,1,0:T(8,128)S(1)}, u32[]{:S(2)}, u32[]{:S(2)}) collective-permute-start(f32[2,3,32,128]{3,2,1,0:T(8,128)S(1)} %get-tuple-element.21), channel_id=1, source_target_pairs={{32,0},{64,32},{96,64},{128,96},{160,128},{192,160},{224,192},{33,... | collective-permute-start | bytes 294920 | tf_op jit(solution)/shard_map/ppermute | solution.py:23
  7.2 3.5 %collective-permute-start = (f32[2,3,32,128]{3,2,1,0:T(8,128)S(1)}, f32[2,3,32,128]{3,2,1,0:T(8,128)S(1)}, u32[]{:S(2)}, u32[]{:S(2)}) collective-permute-start(f32[2,3,32,128]{3,2,1,0:T(8,128)S(1)} %get-tuple-element.20), channel_id=1, source_target_pairs={{0,32},{32,64},{64,96},{96,128},{128,160},{160,192},{192,224},{1,3... | collective-permute-start | bytes 294920 | tf_op jit(solution)/shard_map/ppermute | solution.py:22
  10.8 7.7 %collective-permute-start.3 = (f32[2,38,3,128]{3,2,1,0:T(4,128)S(1)}, f32[2,38,3,128]{3,2,1,0:T(4,128)S(1)}, u32[]{:S(2)}, u32[]{:S(2)}) collective-permute-start(f32[2,38,3,128]{3,2,1,0:T(4,128)S(1)} %get-tuple-element.19), channel_id=1, source_target_pairs={{1,0},{2,1},{3,2},{4,3},{5,4},{6,5},{7,6},{8,7},{9,8},{10,9},{11,1... | collective-permute-start | bytes 350216 | tf_op jit(solution)/shard_map/ppermute | solution.py:23
  12.1 7.4 %collective-permute-start.2 = (f32[2,38,3,128]{3,2,1,0:T(4,128)S(1)}, f32[2,38,3,128]{3,2,1,0:T(4,128)S(1)}, u32[]{:S(2)}, u32[]{:S(2)}) collective-permute-start(f32[2,38,3,128]{3,2,1,0:T(4,128)S(1)} %get-tuple-element.18), channel_id=1, source_target_pairs={{0,1},{1,2},{2,3},{3,4},{4,5},{5,6},{6,7},{7,8},{8,9},{9,10},{10,1... | collective-permute-start | bytes 350216 | tf_op jit(solution)/shard_map/ppermute | solution.py:22
  20.4 3.1 copy-start.1
  20.5 3.1 copy-start.3
  20.5 3.1 copy-start.5
  20.5 1.4 copy-start.9
  24.2 171.6 %collective-permute-start.5 = (f32[2,32,128]{2,1,0:T(8,128)}, f32[2,32,128]{2,1,0:T(8,128)S(1)}, u32[]{:S(2)}, u32[]{:S(2)}) collective-permute-start(f32[2,32,128]{2,1,0:T(8,128)} %get-tuple-element.33), channel_id=1, source_target_pairs={{32,0},{64,32},{96,64},{128,96},{160,128},{192,160},{224,192},{33,... | collective-permute-start | bytes 98312 | tf_op jit(solution)/shard_map/ppermute | solution.py:23
  27.0 168.8 %collective-permute-start.4 = (f32[2,32,128]{2,1,0:T(8,128)}, f32[2,32,128]{2,1,0:T(8,128)S(1)}, u32[]{:S(2)}, u32[]{:S(2)}) collective-permute-start(f32[2,32,128]{2,1,0:T(8,128)} %get-tuple-element.32), channel_id=1, source_target_pairs={{0,32},{32,64},{64,96},{96,128},{128,160},{160,192},{192,224},{1,3... | collective-permute-start | bytes 98312 | tf_op jit(solution)/shard_map/ppermute | solution.py:22
  196.4 11.3 %collective-permute-start.7 = (f32[36,2,128]{2,1,0:T(2,128)}, f32[36,2,128]{2,1,0:T(2,128)}, u32[]{:S(2)}, u32[]{:S(2)}) collective-permute-start(f32[36,2,128]{2,1,0:T(2,128)} %get-tuple-element.27), channel_id=1, source_target_pairs={{1,0},{2,1},{3,2},{4,3},{5,4},{6,5},{7,6},{8,7},{9,8},{10,9},{11,1... | collective-permute-start | bytes 110600 | tf_op jit(solution)/shard_map/ppermute | solution.py:23
  197.7 10.0 %collective-permute-start.6 = (f32[36,2,128]{2,1,0:T(2,128)}, f32[36,2,128]{2,1,0:T(2,128)}, u32[]{:S(2)}, u32[]{:S(2)}) collective-permute-start(f32[36,2,128]{2,1,0:T(2,128)} %get-tuple-element.26), channel_id=1, source_target_pairs={{0,1},{1,2},{2,3},{3,4},{4,5},{5,6},{6,7},{7,8},{8,9},{9,10},{10,1... | collective-permute-start | bytes 110600 | tf_op jit(solution)/shard_map/ppermute | solution.py:22
  207.8 1.2 copy-start.6
  208.8 1.1 copy-start.2
  208.8 1.4 copy-start.4
  214.1 0.7 copy-start.10
  215.3 15.6 %copy-start.7 = (f32[32,32,128]{2,1,0:T(8,128)}, f32[32,32,128]{2,1,0:T(8,128)S(1)}, u32[]{:S(2)}) copy-start(f32[32,32,128]{2,1,0:T(8,128)S(1)} %fusion.40) | copy-start | bytes 1572868
  215.4 5.6 %collective-permute-start.9 = (f32[1,32,128]{2,1,0:T(8,128)S(1)}, f32[1,32,128]{2,1,0:T(8,128)S(1)}, u32[]{:S(2)}, u32[]{:S(2)}) collective-permute-start(f32[1,32,128]{2,1,0:T(8,128)S(1)} %get-tuple-element.31), channel_id=1, source_target_pairs={{32,0},{64,32},{96,64},{128,96},{160,128},{192,160},{224,192},{33,... | collective-permute-start | bytes 49160 | tf_op jit(solution)/shard_map/ppermute | solution.py:23
  218.5 3.3 %collective-permute-start.8 = (f32[1,32,128]{2,1,0:T(8,128)S(1)}, f32[1,32,128]{2,1,0:T(8,128)S(1)}, u32[]{:S(2)}, u32[]{:S(2)}) collective-permute-start(f32[1,32,128]{2,1,0:T(8,128)S(1)} %get-tuple-element.30), channel_id=1, source_target_pairs={{0,32},{32,64},{64,96},{96,128},{128,160},{160,192},{192,224},{1,3... | collective-permute-start | bytes 49160 | tf_op jit(solution)/shard_map/ppermute | solution.py:22
  221.8 5.3 %collective-permute-start.11 = (f32[34,1,128]{2,1,0:T(1,128)S(1)}, f32[34,1,128]{2,1,0:T(1,128)S(1)}, u32[]{:S(2)}, u32[]{:S(2)}) collective-permute-start(f32[34,1,128]{2,1,0:T(1,128)S(1)} %get-tuple-element.29), channel_id=1, source_target_pairs={{1,0},{2,1},{3,2},{4,3},{5,4},{6,5},{7,6},{8,7},{9,8},{10,9},{11,1... | collective-permute-start | bytes 52232 | tf_op jit(solution)/shard_map/ppermute | solution.py:23
  223.1 4.9 %collective-permute-start.10 = (f32[34,1,128]{2,1,0:T(1,128)S(1)}, f32[34,1,128]{2,1,0:T(1,128)S(1)}, u32[]{:S(2)}, u32[]{:S(2)}) collective-permute-start(f32[34,1,128]{2,1,0:T(1,128)S(1)} %get-tuple-element.28), channel_id=1, source_target_pairs={{0,1},{1,2},{2,3},{3,4},{4,5},{5,6},{6,7},{7,8},{8,9},{9,10},{10,1... | collective-permute-start | bytes 52232 | tf_op jit(solution)/shard_map/ppermute | solution.py:22
where the time goes:
time: 318 us; the launch traced here: 317 us
  blocking collectives  238 us (75%)
  starting transfers between devices  35.2 us (11%)
  other arithmetic  18 us (6%)
  local copies, waits for them, and re-layouts  13.8 us (4%)
  waiting for transfers between devices  4.82 us (2%)
  matrix products  4.28 us (1%)
    psum x1, blocking collectives, body(): coarse_resid = lax.psum(partial_resid, ('gx', 'gy'))  83.7 us
    psum x1, blocking collectives, body(): lax.psum((jnp.sum(resid * direction), jnp.sum(direction * image)), ('gx',...  81.9 us
    unnamed x1, blocking collectives  72.7 us
    ppermute x6, starting transfers between devices, with_halo(): before = lax.ppermute(last, axis, up)  20.3 us
    ppermute x6, starting transfers between devices, with_halo(): after = lax.ppermute(initial, axis, down)  14.9 us
  transfers between devices with their start and end apart: 12, of which 5 were waited for; matrix products, arithmetic and copies ran while one was open for 5% of the time, Pallas kernels for 0%

commit v1 on v0

v1 whole, which is shorter than its diff:
```python
import jax
import jax.numpy as jnp
from jax import lax
from jax.experimental import pallas as pl
from jax.experimental.pallas import tpu as pltpu
from jax.sharding import PartitionSpec as P

F32 = jnp.float32
MESH = pl.DeviceIdType.MESH
BLK = 16
T = 32
NZ = 128
SWEEPS = 4
STRIDE = 40
ROWS = 40
FLAT = ROWS * STRIDE
NODES = 1024
GROUP = 16
screen = 0.02
relax = 0.8
LO, CHUNK, STEPS = 72, 112, 13


def flat_of(x, y):
    return (x + 4) * STRIDE + y


def view(ref):
    return ref.reshape(FLAT, NZ)


def kernel(
    cmap, cinv, right, guess, conductivity, wet,
    d_out, image_out, resid_out, alpha_out,
    ext, mask, w_east, w_north, w_above, diag, dinv, first, e_a, e_b, resid, d_ext, image, inverse,
    ya_send, ya_recv, yb_send, yb_recv, k_send, k_recv, map_send, map_recv, l_send, l_recv,
    part, recv,
    load_sem, out_sem, xa_ss, xa_rs, xb_ss, xb_rs, xr_ss, xr_rs, ya_ss, ya_rs, yb_ss, yb_rs,
    k_ss, k_rs, map_ss, map_rs, l_ss, l_rs, g_ss, g_rs,
):
    gx, gy = lax.axis_index("gx"), lax.axis_index("gy")
    n_gx, n_gy = lax.axis_size("gx"), lax.axis_size("gy")
    west = (lax.rem(gx + n_gx - 1, n_gx), gy)
    east = (lax.rem(gx + 1, n_gx), gy)
    south = (gx, lax.rem(gy + n_gy - 1, n_gy))
    north = (gx, lax.rem(gy + 1, n_gy))
    corners = [(px[0], py[1]) for px in (west, east) for py in (south, north)]
    sides = (west, east, south, north)
    near = gx * 2 + lax.rem(gy, 2)
    far = gy // 2

    def near_peer(k):
        j = lax.rem(near + k, GROUP)
        return (j // 2, far * 2 + lax.rem(j, 2))

    def far_peer(k):
        j = lax.rem(far + k, GROUP)
        return (gx, j * 2 + lax.rem(gy, 2))

    own = (pl.ds(4, T), pl.ds(0, T))
    loads = [
        pltpu.make_async_copy(conductivity, ext.at[(0,) + own], load_sem.at[0]),
        pltpu.make_async_copy(wet, mask, load_sem.at[1]),
        pltpu.make_async_copy(guess, ext.at[(1,) + own], load_sem.at[2]),
        pltpu.make_async_copy(right, ext.at[(2,) + own], load_sem.at[3]),
        pltpu.make_async_copy(cinv, inverse, load_sem.at[4]),
    ]
    for copy in loads:
        copy.start()

    pad = jnp.zeros((8, NZ), F32)
    wide = jnp.zeros((STRIDE, NZ), F32)
    for a in range(3):
        for r in (0, 1, 2, 3, 36, 37, 38, 39):
            ext[a, r] = wide
        for r in range(4, 36):
            ext[a, r, pl.ds(32, 8)] = pad
    for ref in (w_east, w_north, first, e_a, e_b):
        view(ref)[pl.ds(0, LO)] = jnp.zeros((LO, NZ), F32)
        view(ref)[pl.ds(LO + CHUNK * STEPS, FLAT - LO - CHUNK * STEPS)] = jnp.zeros(
            (FLAT - LO - CHUNK * STEPS, NZ), F32)

    barrier = pltpu.get_barrier_semaphore()
    for peer in list(sides) + corners:
        pl.semaphore_signal(barrier, inc=1, device_id=peer, device_id_type=MESH)

    def greet(k, carry):
        pl.semaphore_signal(barrier, inc=1, device_id=near_peer(k), device_id_type=MESH)
        pl.semaphore_signal(barrier, inc=1, device_id=far_peer(k), device_id_type=MESH)
        return carry

    lax.fori_loop(1, GROUP, greet, 0)

    sub = lax.broadcasted_iota(jnp.int32, (8, NZ), 0)
    lane = lax.broadcasted_iota(jnp.int32, (8, NZ), 1)
    node_of = sub * NZ + lane
    nodes = [[cmap[bx, by, 0] for by in range(2)] for bx in range(2)]
    packed = jnp.zeros((8, NZ), jnp.int32)
    for bx in range(2):
        for by in range(2):
            packed = jnp.where(sub == 2 * bx + by, nodes[bx][by], packed)
    map_send[...] = packed

    def remote(src, dst, ss, rs, peer):
        return pltpu.make_async_remote_copy(
            src_ref=src, dst_ref=dst, send_sem=ss, recv_sem=rs, device_id=peer, device_id_type=MESH)

    loads[0].wait()
    loads[1].wait()

    def masked(r, carry):
        ext[0, r + 4, pl.ds(0, T)] = ext[0, r + 4, pl.ds(0, T)] * mask[r].astype(F32)
        return carry

    lax.fori_loop(0, T, masked, 0, unroll=4)
    loads[2].wait()
    cond_f, guess_f, right_f = (view(ext.at[a]) for a in range(3))
    fields = (cond_f, guess_f)

    def column(ref, y):
        return ref[pl.ds(flat_of(0, y), T, stride=STRIDE)]

    for a in range(2):
        ya_send[0, a] = column(fields[a], 0)
        ya_send[1, a] = column(fields[a], T - 1)
    pl.semaphore_wait(barrier, 8 + 2 * (GROUP - 1))

    x_from, x_to = (4, 35), (36, 3)
    started = []

    def start(copy):
        copy.start()
        started.append(copy)
        return copy

    xa = [start(remote(ext.at[pl.ds(0, 2), x_from[s], pl.ds(0, T)], ext.at[pl.ds(0, 2), x_to[s], pl.ds(0, T)],
                       xa_ss.at[s], xa_rs.at[s], sides[s])) for s in range(2)]
    ya = [start(remote(ya_send.at[s], ya_recv.at[s], ya_ss.at[s], ya_rs.at[s], sides[2 + s])) for s in range(2)]
    loads[3].wait()
    for s, rows in enumerate(((1, 2), (T - 3, T - 2))):
        for a in range(2):
            for i in range(2):
                yb_send[s, 2 * a + i] = column(fields[a], rows[i])
    for s, rows in enumerate(((0, 1), (T - 2, T - 1))):
        for i in range(2):
            yb_send[s, 4 + i] = column(right_f, rows[i])
    xb_from, xb_to = (5, 33), (37, 1)
    xr_from, xr_to = (4, 34), (36, 2)
    xb, xr = [], []
    for s in range(2):
        xb.append(start(remote(ext.at[pl.ds(0, 2), pl.ds(xb_from[s], 2), pl.ds(0, T)],
                               ext.at[pl.ds(0, 2), pl.ds(xb_to[s], 2), pl.ds(0, T)],
                               xb_ss.at[s], xb_rs.at[s], sides[s])))
        xr.append(start(remote(ext.at[2, pl.ds(xr_from[s], 2), pl.ds(0, T)],
                               ext.at[2, pl.ds(xr_to[s], 2), pl.ds(0, T)],
                               xr_ss.at[s], xr_rs.at[s], sides[s])))
    yb = [start(remote(yb_send.at[s], yb_recv.at[s], yb_ss.at[s], yb_rs.at[s], sides[2 + s])) for s in range(2)]
    kc = []
    for q in range(4):
        sx, sy = q // 2, q % 2
        x3, y3 = (0, T - 3)[sx], (0, T - 3)[sy]
        x2, y2 = (0, T - 2)[sx], (0, T - 2)[sy]
        for a in range(2):
            for i in range(3):
                k_send[q, pl.ds(9 * a + 3 * i, 3)] = fields[a][pl.ds(flat_of(x3 + i, y3), 3)]
        k_send[q, pl.ds(22, 2)] = jnp.zeros((2, NZ), F32)
        for i in range(2):
            k_send[q, pl.ds(18 + 2 * i, 2)] = right_f[pl.ds(flat_of(x2 + i, y2), 2)]
        kc.append(start(remote(k_send.at[q], k_recv.at[q], k_ss.at[q], k_rs.at[q], corners[q])))
    mc = [start(remote(map_send, map_recv.at[s], map_ss.at[s], map_rs.at[s], sides[s])) for s in range(4)]

    def cells(bx):
        def add(r, acc):
            c = ext[0, 4 + 16 * bx + r, pl.ds(0, T)]
            g = ext[1, 4 + 16 * bx + r, pl.ds(0, T)]
            b = ext[2, 4 + 16 * bx + r, pl.ds(0, T)]
            return acc + (b - (screen + jnp.maximum(0.0, 1.0 - 2.0 * c)) * g)
        return lax.fori_loop(0, BLK, add, jnp.zeros((T, NZ), F32), unroll=4)

    def halves(v):
        return v[:BLK], v[BLK:]

    sums = [list(halves(cells(0))), list(halves(cells(1)))]

    def flux(c0, g0, c1, g1):
        return halves(jnp.minimum(c0, c1) * (g0 - g1))

    def row(a, x):
        return ext[a, 4 + x, pl.ds(0, T)]

    mid = flux(row(0, 15), row(1, 15), row(0, 16), row(1, 16))
    for i in range(2):
        sums[0][i] -= mid[i]
        sums[1][i] += mid[i]
    mid = flux(column(cond_f, 15), column(guess_f, 15), column(cond_f, 16), column(guess_f, 16))
    for i in range(2):
        sums[i][0] -= mid[i]
        sums[i][1] += mid[i]

    def clear(rows):
        cond_f[pl.ds(rows[0], rows[1])] = jnp.zeros((rows[1], NZ), F32)

    for s in range(2):
        xa[s].wait_recv()

    @pl.when(gx == 0)
    def _():
        clear((flat_of(-1, 0), T))

    @pl.when(gx == n_gx - 1)
    def _():
        clear((flat_of(T, 0), T))

    for s in range(2):
        ya[s].wait_recv()
    for a in range(2):
        fields[a][pl.ds(flat_of(0, T), T, stride=STRIDE)] = ya_recv[0, a]
        fields[a][pl.ds(flat_of(0, -1), T, stride=STRIDE)] = ya_recv[1, a]

    @pl.when(gy == 0)
    def _():
        cond_f[pl.ds(flat_of(0, -1), T, stride=STRIDE)] = jnp.zeros((T, NZ), F32)

    @pl.when(gy == n_gy - 1)
    def _():
        cond_f[pl.ds(flat_of(0, T), T, stride=STRIDE)] = jnp.zeros((T, NZ), F32)

    edge_x = [flux(row(0, x), row(1, x), row(0, n), row(1, n)) for x, n in ((0, -1), (T - 1, T))]
    edge_y = [flux(column(cond_f, y), column(guess_f, y), column(cond_f, n), column(guess_f, n))
              for y, n in ((0, -1), (T - 1, T))]
    vec = jnp.zeros((8, NZ), F32)
    for bx in range(2):
        for by in range(2):
            total = sums[bx][by] - edge_x[bx][by] - edge_y[by][bx]
            total = jnp.sum(jnp.sum(total, axis=0, keepdims=True), axis=1, keepdims=True)
            vec = vec + jnp.where(node_of == nodes[bx][by], total, 0.0)

    def send_group(stage, value, peer_of):
        part[stage] = value
        for k in range(1, GROUP):
            remote(part.at[stage], recv.at[stage, GROUP - 1 - k], g_ss.at[stage], g_rs.at[stage], peer_of(k)).start()

    def recv_group(stage):
        pltpu.make_async_copy(recv.at[stage], recv.at[stage], g_rs.at[stage]).wait()
        return part[stage] + jnp.sum(recv[stage], axis=0)

    send_group(0, vec, near_peer)

    for s in range(2):
        xb[s].wait_recv()
        xr[s].wait_recv()
        yb[s].wait_recv()
    for s, rows in enumerate(((T + 1, T + 2), (-3, -2))):
        for a in range(2):
            for i in range(2):
                fields[a][pl.ds(flat_of(0, rows[i]), T, stride=STRIDE)] = yb_recv[s, 2 * a + i]
    for s, rows in enumerate(((T, T + 1), (-2, -1))):
        for i in range(2):
            right_f[pl.ds(flat_of(0, rows[i]), T, stride=STRIDE)] = yb_recv[s, 4 + i]
    for q in range(4):
        kc[q].wait_recv()
        sx, sy = q // 2, q % 2
        x3, y3 = (T, -3)[sx], (T, -3)[sy]
        x2, y2 = (T, -2)[sx], (T, -2)[sy]
        for a in range(2):
            for i in range(3):
                fields[a][pl.ds(flat_of(x3 + i, y3), 3)] = k_recv[q, pl.ds(9 * a + 3 * i, 3)]
        for i in range(2):
            right_f[pl.ds(flat_of(x2 + i, y2), 2)] = k_recv[q, pl.ds(18 + 2 * i, 2)]

    @pl.when(gx == 0)
    def _():
        clear((flat_of(-3, -4), 3 * STRIDE))

    @pl.when(gx == n_gx - 1)
    def _():
        clear((flat_of(T, -4), 3 * STRIDE))

    @pl.when(gy == 0)
    def _():
        for y in (-3, -2, -1):
            cond_f[pl.ds(flat_of(-3, y), T + 6, stride=STRIDE)] = jnp.zeros((T + 6, NZ), F32)

    @pl.when(gy == n_gy - 1)
    def _():
        for y in (T, T + 1, T + 2):
            cond_f[pl.ds(flat_of(-3, y), T + 6, stride=STRIDE)] = jnp.zeros((T + 6, NZ), F32)

    w_east_f, w_north_f, w_above_f, diag_f, dinv_f, first_f, resid_f, e_a_f, e_b_f, d_f = (
        view(ref) for ref in (w_east, w_north, w_above, diag, dinv, first, resid, e_a, e_b, d_ext))
    top = lax.broadcasted_iota(jnp.int32, (CHUNK, NZ), 1) == NZ - 1

    def up(v):
        return pltpu.roll(v, NZ - 1, 1)

    def down(v):
        return pltpu.roll(v, 1, 1)

    def prepare(i, carry):
        f = pl.multiple_of(LO + i * CHUNK, 8)
        at = pl.ds(f, CHUNK)
        c = cond_f[at]
        g = guess_f[at]
        we = jnp.minimum(c, cond_f[pl.ds(f + STRIDE, CHUNK)])
        ww = jnp.minimum(c, cond_f[pl.ds(f - STRIDE, CHUNK)])
        wn = jnp.minimum(c, cond_f[pl.ds(f + 1, CHUNK)])
        ws = jnp.minimum(c, cond_f[pl.ds(f - 1, CHUNK)])
        wa = jnp.where(top, 0.0, jnp.minimum(c, up(c)))
        wb = down(wa)
        w_east_f[at] = we
        w_north_f[at] = wn
        w_above_f[at] = wa
        dg = screen + jnp.maximum(0.0, 1.0 - 2.0 * c) + ww + we + ws + wn + wb + wa
        diag_f[at] = dg
        total = ww * guess_f[pl.ds(f - STRIDE, CHUNK)] + we * guess_f[pl.ds(f + STRIDE, CHUNK)]
        total = total + ws * guess_f[pl.ds(f - 1, CHUNK)] + wn * guess_f[pl.ds(f + 1, CHUNK)]
        total = total + down(wa * g) + wa * up(g)
        r = right_f[at] - dg * g + total
        resid_f[at] = r
        di = relax / dg
        dinv_f[at] = di
        first_f[at] = di * r
        return carry

    lax.fori_loop(0, STEPS, prepare, 0)
    for ref in (dinv_f, first_f):
        ref[pl.ds(flat_of(-3, 32), 6)] = jnp.zeros((6, NZ), F32)
        for x in range(-2, 33):
            ref[pl.ds(flat_of(x, 34), 4)] = jnp.zeros((4, NZ), F32)
        last = flat_of(33, 34)
        ref[pl.ds(last, LO + CHUNK * STEPS - last)] = jnp.zeros((LO + CHUNK * STEPS - last, NZ), F32)

    @pl.when(gx == 0)
    def _():
        first_f[pl.ds(flat_of(-2, -4), 2 * STRIDE)] = jnp.zeros((2 * STRIDE, NZ), F32)

    @pl.when(gx == n_gx - 1)
    def _():
        first_f[pl.ds(flat_of(T, -4), 2 * STRIDE)] = jnp.zeros((2 * STRIDE, NZ), F32)

    @pl.when(gy == 0)
    def _():
        for y in (-2, -1):
            first_f[pl.ds(flat_of(-2, y), T + 4, stride=STRIDE)] = jnp.zeros((T + 4, NZ), F32)

    @pl.when(gy == n_gy - 1)
    def _():
        for y in (T, T + 1):
            first_f[pl.ds(flat_of(-2, y), T + 4, stride=STRIDE)] = jnp.zeros((T + 4, NZ), F32)

    def around(ref, f, n):
        at = pl.ds(f, n)
        v = ref[at]
        wa = w_above_f[at]
        total = w_east_f[at] * ref[pl.ds(f + STRIDE, n)]
        total = total + w_east_f[pl.ds(f - STRIDE, n)] * ref[pl.ds(f - STRIDE, n)]
        total = total + w_north_f[at] * ref[pl.ds(f + 1, n)]
        total = total + w_north_f[pl.ds(f - 1, n)] * ref[pl.ds(f - 1, n)]
        return total + wa * up(v) + down(wa * v), v

    def sweep(src, dst):
        def step(i, carry):
            f = pl.multiple_of(LO + i * CHUNK, 8)
            at = pl.ds(f, CHUNK)
            total, v = around(src, f, CHUNK)
            dst[at] = (1.0 - relax) * v + first_f[at] + dinv_f[at] * total
            return carry
        lax.fori_loop(0, STEPS, step, 0)

    send_group(1, recv_group(0), far_peer)
    sweep(first_f, e_a_f)

    loads[4].wait()
    coarse_resid = recv_group(1)
    acc = jnp.zeros((4, NZ), F32)
    for k in range(8):
        acc = acc + inverse[:, pl.ds(NZ * k, NZ)] * coarse_resid[k:k + 1]
    acc = jnp.sum(acc, axis=1, keepdims=True)
    vec = jnp.zeros((8, NZ), F32)
    base = (gx * n_gy + gy) * 4
    for i in range(4):
        vec = vec + jnp.where(node_of == base + i, acc[i:i + 1], 0.0)
    send_group(2, vec, near_peer)
    sweep(e_a_f, e_b_f)
    send_group(3, recv_group(2), far_peer)
    sweep(e_b_f, e_a_f)
    l_send[0] = row_of(e_a, 0)
    l_send[1] = row_of(e_a, T - 1)
    l_send[2] = column(e_a_f, 0)
    l_send[3] = column(e_a_f, T - 1)
    lc = [start(remote(l_send.at[s], l_recv.at[s], l_ss.at[s], l_rs.at[s], sides[s])) for s in range(4)]

    coarse = recv_group(3)

    def lookup(node):
        found = jnp.where(node_of == node, coarse, 0.0)
        return jnp.sum(jnp.sum(found, axis=0, keepdims=True), axis=1, keepdims=True)

    high = lax.broadcasted_iota(jnp.int32, (T, NZ), 0) >= BLK

    def spread(lower, upper):
        return jnp.where(high, upper, lower)

    mine = [spread(lookup(nodes[bx][0]), lookup(nodes[bx][1])) for bx in range(2)]
    for bx in range(2):
        def place(r, carry):
            d_ext[4 + BLK * bx + r, pl.ds(0, T)] = e_a[4 + BLK * bx + r, pl.ds(0, T)] + mine[bx]
            return carry
        lax.fori_loop(0, BLK, place, 0, unroll=4)
    for s in range(4):
        mc[s].wait_recv()
        lc[s].wait_recv()
    pairs = ((0, 1), (2, 3), (0, 2), (1, 3))
    beside = []
    for s in range(4):
        ids = map_recv[s]
        beside.append(spread(*(lookup(ids[p:p + 1]) for p in pairs[s])) + l_recv[s])
    d_ext[36, pl.ds(0, T)] = beside[0]
    d_ext[3, pl.ds(0, T)] = beside[1]
    d_f[pl.ds(flat_of(0, T), T, stride=STRIDE)] = beside[2]
    d_f[pl.ds(flat_of(0, -1), T, stride=STRIDE)] = beside[3]

    def apply(x, carry):
        numer, denom = carry
        f = pl.multiple_of((x + 4) * STRIDE, 8)
        total, v = around(d_f, f, T)
        im = diag_f[pl.ds(f, T)] * v - total
        image[x] = im
        return numer + resid_f[pl.ds(f, T)] * v, denom + v * im

    zero = jnp.zeros((T, NZ), F32)
    numer, denom = lax.fori_loop(0, T, apply, (zero, zero), unroll=2)
    outs = [
        pltpu.make_async_copy(d_ext.at[own], d_out, out_sem.at[0]),
        pltpu.make_async_copy(image, image_out, out_sem.at[1]),
        pltpu.make_async_copy(resid.at[own], resid_out, out_sem.at[2]),
    ]
    for copy in outs:
        copy.start()
    numer = jnp.sum(numer, axis=0, keepdims=True)
    denom = jnp.sum(denom, axis=0, keepdims=True)
    send_group(4, jnp.where(sub == 0, numer, jnp.where(sub == 1, denom, 0.0)), near_peer)
    send_group(5, recv_group(4), far_peer)
    both = jnp.sum(recv_group(5), axis=1, keepdims=True)
    alpha_out[...] = jnp.broadcast_to(both[0:1] / both[1:2], (8, NZ))

    for copy in started:
        copy.wait_send()
    for stage in range(6):
        pltpu.make_async_copy(recv.at[stage], recv.at[stage], g_ss.at[stage]).wait()
    for copy in outs:
        copy.wait()


def row_of(ref, x):
    return ref[4 + x, pl.ds(0, T)]


def body(right_side, guess, conductivity, wet_mask, coarse_map, coarse_inverse):
    tile = jax.ShapeDtypeStruct((T, T, NZ), F32)
    anywhere = pl.BlockSpec(memory_space=pl.ANY)
    field = pltpu.VMEM((ROWS, STRIDE, NZ), F32)
    dma = pltpu.SemaphoreType.DMA
    d, image, resid, alpha = pl.pallas_call(
        kernel,
        out_shape=(tile, tile, tile, jax.ShapeDtypeStruct((8, NZ), F32)),
        in_specs=[pl.BlockSpec(memory_space=pltpu.SMEM)] + [anywhere] * 5,
        out_specs=(anywhere, anywhere, anywhere, pl.BlockSpec(memory_space=pltpu.VMEM)),
        scratch_shapes=[
            pltpu.VMEM((3, ROWS, STRIDE, NZ), F32), pltpu.VMEM((T, T, NZ), jnp.int32),
        ] + [field] * 10 + [
            pltpu.VMEM((T, T, NZ), F32), pltpu.VMEM((4, NODES), F32),
            pltpu.VMEM((2, 2, T, NZ), F32), pltpu.VMEM((2, 2, T, NZ), F32),
            pltpu.VMEM((2, 6, T, NZ), F32), pltpu.VMEM((2, 6, T, NZ), F32),
            pltpu.VMEM((4, 24, NZ), F32), pltpu.VMEM((4, 24, NZ), F32),
            pltpu.VMEM((8, NZ), jnp.int32), pltpu.VMEM((4, 8, NZ), jnp.int32),
            pltpu.VMEM((4, T, NZ), F32), pltpu.VMEM((4, T, NZ), F32),
            pltpu.VMEM((6, 8, NZ), F32), pltpu.VMEM((6, GROUP - 1, 8, NZ), F32),
            dma((5,)), dma((3,)),
        ] + [dma((2,))] * 10 + [dma((4,))] * 6 + [dma((6,))] * 2,
        compiler_params=pltpu.CompilerParams(
            collective_id=0, has_side_effects=True, vmem_limit_bytes=40 * 1024 * 1024),
    )(coarse_map, coarse_inverse, right_side, guess, conductivity, wet_mask)
    step = alpha[0, 0]
    return guess + step * d, resid - step * image


def solution(mesh):
    grid = P("gx", "gy", None)
    in_specs = (grid, grid, grid, grid, grid, P(("gx", "gy"), None))
    return jax.shard_map(body, mesh=mesh, in_specs=in_specs, out_specs=(grid, grid), check_vma=False)
```

time: 318 us -> 59.9 us (0.19)
  blocking collectives: 238 us -> 0 us
  Pallas kernels: 0 us -> 50.8 us
  starting transfers between devices: 35.2 us -> 0 us
  other arithmetic: 18 us -> 1.88 us
  local copies, waits for them, and re-layouts: 13.8 us -> 6.24 us
  waiting for transfers between devices: 4.82 us -> 0 us
  matrix products: 4.28 us -> 0 us
    psum x2 -> x0, blocking collectives: 166 us -> none  [the longest x1 83.7 us: body(): coarse_resid = lax.psum(partial_resid, ('gx', 'gy'))]
    unnamed x1 -> x0, blocking collectives: 72.7 us -> none
    pallas_call x0 -> x1, Pallas kernels: none -> 50.8 us  [body(): pl.pallas_call(kernel, out_shape=(tile, tile, tile, jax.ShapeDtypeStruct(...]
    ppermute x12 -> x0, starting transfers between devices: 35.2 us -> none  [the longest x6 20.3 us: with_halo(): before = lax.ppermute(last, axis, up)]
    reduce_sum x3 -> x0, other arithmetic: 5.51 us -> none  [the longest x2 3.1 us: body(): resid.reshape(blocks_x, BLK, blocks_y, BLK, levels).sum(axis=(1, 3, 4))]
    add x5 -> x0, other arithmetic: 4.9 us -> none  [the longest x2 3.38 us: smooth(): correction + relax * (resid - diag * correction + neighbours(padded, weig...]
    ppermute x12 -> x0, waiting for transfers between devices: 4.82 us -> none  [the longest x6 4.29 us: with_halo(): before = lax.ppermute(last, axis, up)]
    dot_general x3 -> x0, matrix products: 4.28 us -> none  [the longest x1 1.46 us: body(): partial_resid = jnp.dot(block_sums, onehot, precision=lax.Precision.HIGHEST)]
  transfers between devices with their start and end apart: 12 -> 0, of which waited for: 5 -> 0; matrix products, arithmetic and copies ran while one was open for 5% -> 0% of each run, Pallas kernels for 0% -> 0%
where the time goes in v1:
time: 59.9 us; the launch traced here: 59.5 us
  Pallas kernels  50.8 us (85%)
  local copies, waits for them, and re-layouts  6.24 us (10%)
  other arithmetic  1.88 us (3%)
  between operations  0.64 us (1%)
    pallas_call x1, Pallas kernels, body(): pl.pallas_call(kernel, out_shape=(tile, tile, tile, jax.ShapeDtypeStruct(...  50.8 us
    unnamed x11, local copies, waits for them, and re-layouts  5.65 us
    sub x1, other arithmetic, body(): return (guess + step * d, resid - step * image)  1.88 us

profile of v1, /device:TPU:1, one launch (start us, length us, event | category | flops | bytes accessed | tf_op | source)
XLA Modules:
  0.0 59.5 jit_solution(11824779342718623746)
XLA Ops:
  0.6 0.8 %copy.8.cmap = s32[2,2,1]{2,1,0:T(2,128)S(1)} copy(s32[2,2,1]{1,2,0:T(1,128)} %param.10) | data formatting | bytes 32 | tf_op args[4]
  1.4 0.0 copy-start
  1.4 1.0 %copy-done = f32[32,32,128]{2,1,0:T(8,128)S(1)} copy-done((f32[32,32,128]{2,1,0:T(8,128)S(1)}, f32[32,32,128]{2,1,0:T(8,128)}, u32[]{:S(2)}) %copy-start) | copy-done | bytes 524312
  2.4 0.0 copy-start.1
  2.4 1.0 %copy-done.1 = f32[32,32,128]{2,1,0:T(8,128)S(1)} copy-done((f32[32,32,128]{2,1,0:T(8,128)S(1)}, f32[32,32,128]{2,1,0:T(8,128)}, u32[]{:S(2)}) %copy-start.1) | copy-done | bytes 524312
  3.5 0.0 copy-start.2
  3.5 1.0 %copy-done.2 = f32[32,32,128]{2,1,0:T(8,128)S(1)} copy-done((f32[32,32,128]{2,1,0:T(8,128)S(1)}, f32[32,32,128]{2,1,0:T(8,128)}, u32[]{:S(2)}) %copy-start.2) | copy-done | bytes 524312
  4.5 0.0 copy-start.3
  4.5 1.0 %copy-done.3 = s32[32,32,128]{2,1,0:T(8,128)S(1)} copy-done((s32[32,32,128]{2,1,0:T(8,128)S(1)}, s32[32,32,128]{2,1,0:T(8,128)}, u32[]{:S(2)}) %copy-start.3) | copy-done | bytes 524312
  5.6 0.0 copy-start.4
  5.6 0.7 %copy-done.4 = f32[4,1024]{1,0:T(4,128)S(1)} copy-done((f32[4,1024]{1,0:T(4,128)S(1)}, f32[4,1024]{1,0:T(4,128)}, u32[]{:S(2)}) %copy-start.4) | copy-done | bytes 16408
  6.3 50.8 %shard_map.77 = (f32[32,32,128]{2,1,0:T(8,128)S(1)}, f32[32,32,128]{2,1,0:T(8,128)S(1)}, f32[32,32,128]{2,1,0:T(8,128)S(1)}, f32[8,128]{1,0:T(8,128)S(1)}) custom-call(s32[2,2,1]{2,1,0:T(2,128)S(1)} %copy.8.cmap, f32[4,1024]{1,0:T(4,128)S(1)} %copy-done.4, f32[32,32,128]{2,1,0:T(8,128)S(1)} %copy-done.1, f32[32,32,128]{2,1,0:T(8,128)S(1)} %copy-done, ...), custom_call_target="tpu_custom_call" | custom-call | tf_op jit(solution)/shard_map/pallas_call | solution.py:464
  57.1 0.6 slice.3
  57.6 1.9 %multiply_subtract_fusion = (f32[32,32,128]{2,1,0:T(8,128)}, f32[32,32,128]{2,1,0:T(8,128)}) fusion(f32[32,32,128]{2,1,0:T(8,128)S(1)} %get-tuple-element.8, f32[32,32,128]{2,1,0:T(8,128)S(1)} %get-tuple-element.9, f32[]{:T(128)} %bitcast, f32[32,32,128]{2,1,0:T(8,128)S(1)} %copy-done, f32[32,32,128]{2,1,0:T(8,128)S(1)} %get-tuple-element.7), kind=kLoop, calls=%fused_computation | loop fusion | flops 524288 | bytes 3145732 | tf_op jit(solution)/shard_map/sub | solution.py:485
Async XLA Ops:
  1.4 1.0 %copy-start = (f32[32,32,128]{2,1,0:T(8,128)S(1)}, f32[32,32,128]{2,1,0:T(8,128)}, u32[]{:S(2)}) copy-start(f32[32,32,128]{2,1,0:T(8,128)} %guess.1) | copy-start | bytes 1572868
  2.4 1.0 %copy-start.1 = (f32[32,32,128]{2,1,0:T(8,128)S(1)}, f32[32,32,128]{2,1,0:T(8,128)}, u32[]{:S(2)}) copy-start(f32[32,32,128]{2,1,0:T(8,128)} %right.1) | copy-start | bytes 1572868
  3.5 1.0 %copy-start.2 = (f32[32,32,128]{2,1,0:T(8,128)S(1)}, f32[32,32,128]{2,1,0:T(8,128)}, u32[]{:S(2)}) copy-start(f32[32,32,128]{2,1,0:T(8,128)} %conductivity.1) | copy-start | bytes 1572868
  4.5 1.0 %copy-start.3 = (s32[32,32,128]{2,1,0:T(8,128)S(1)}, s32[32,32,128]{2,1,0:T(8,128)}, u32[]{:S(2)}) copy-start(s32[32,32,128]{2,1,0:T(8,128)} %wet.1) | copy-start | bytes 1572868
  5.6 0.7 %copy-start.4 = (f32[4,1024]{1,0:T(4,128)S(1)}, f32[4,1024]{1,0:T(4,128)}, u32[]{:S(2)}) copy-start(f32[4,1024]{1,0:T(4,128)} %cinv.1) | copy-start | bytes 49156

commit v2 on v1

v2 whole, which is shorter than its diff:
```python
import jax
import jax.numpy as jnp
from jax import lax
from jax.experimental import pallas as pl
from jax.experimental.pallas import tpu as pltpu
from jax.sharding import PartitionSpec as P

F32 = jnp.float32
MESH = pl.DeviceIdType.MESH
BLK = 16
T = 32
NZ = 128
STRIDE = 40
ROWS = 40
FLAT = ROWS * STRIDE
NODES = 1024
GROUP = 16
screen = 0.02
relax = 0.8
LO, CHUNK, STEPS = 72, 112, 13


def flat_of(x, y):
    return (x + 4) * STRIDE + y


def view(ref):
    return ref.reshape(FLAT, NZ)


def up(v):
    return pltpu.roll(v, NZ - 1, 1)


def down(v):
    return pltpu.roll(v, 1, 1)


def kernel(
    cmap, cinv, right, guess, conductivity, wet,
    d_out, image_out, resid_out, coarse_out, near_out, far_out,
    ext, mask, w_east, w_north, w_above, diag, dinv, first, e_a, e_b, d_ext, inverse,
    a_send, a_recv, b_send, b_recv, k_send, k_recv, l_send, l_recv,
    part, recv,
    load_sem, a_ss, a_rs, b_ss, b_rs, k_ss, k_rs, l_ss, l_rs, g_ss, g_rs,
):
    gx, gy = lax.axis_index("gx"), lax.axis_index("gy")
    n_gx, n_gy = lax.axis_size("gx"), lax.axis_size("gy")
    west = (lax.rem(gx + n_gx - 1, n_gx), gy)
    east = (lax.rem(gx + 1, n_gx), gy)
    south = (gx, lax.rem(gy + n_gy - 1, n_gy))
    north = (gx, lax.rem(gy + 1, n_gy))
    corners = [(px[0], py[1]) for px in (west, east) for py in (south, north)]
    sides = (west, east, south, north)
    near = gx * 2 + lax.rem(gy, 2)
    far = gy // 2

    def near_peer(k):
        j = lax.rem(near + k, GROUP)
        return (j // 2, far * 2 + lax.rem(j, 2))

    def far_peer(k):
        j = lax.rem(far + k, GROUP)
        return (gx, j * 2 + lax.rem(gy, 2))

    near_order = (8, 7, 9, 6, 10, 5, 11, 4, 12, 3, 13, 2, 14, 1, 15)
    far_order = (8, 7, 9, 6, 10, 5, 11, 4, 12, 3, 13, 2, 14, 1, 15)

    barrier = pltpu.get_barrier_semaphore()
    for peer in [far_peer(k) for k in far_order] + [near_peer(k) for k in near_order] + corners + list(sides):
        pl.semaphore_signal(barrier, inc=1, device_id=peer, device_id_type=MESH)

    own = (pl.ds(4, T), pl.ds(0, T))
    loads = [
        pltpu.make_async_copy(conductivity, ext.at[(0,) + own], load_sem.at[0]),
        pltpu.make_async_copy(wet, mask, load_sem.at[1]),
        pltpu.make_async_copy(guess, ext.at[(1,) + own], load_sem.at[2]),
        pltpu.make_async_copy(right, ext.at[(2,) + own], load_sem.at[3]),
        pltpu.make_async_copy(cinv, inverse, load_sem.at[4]),
    ]
    for copy in loads:
        copy.start()

    pad = jnp.zeros((8, NZ), F32)
    wide = jnp.zeros((STRIDE, NZ), F32)
    for a in range(3):
        for r in (0, 1, 2, 3, 36, 37, 38, 39):
            ext[a, r] = wide
        for r in range(4, 36):
            ext[a, r, pl.ds(32, 8)] = pad
    for ref in (w_east, w_north, first, e_a, e_b):
        view(ref)[pl.ds(0, LO)] = jnp.zeros((LO, NZ), F32)
        view(ref)[pl.ds(LO + CHUNK * STEPS, FLAT - LO - CHUNK * STEPS)] = jnp.zeros(
            (FLAT - LO - CHUNK * STEPS, NZ), F32)

    sub = lax.broadcasted_iota(jnp.int32, (8, NZ), 0)
    lane = lax.broadcasted_iota(jnp.int32, (8, NZ), 1)
    node_of = sub * NZ + lane
    nodes = [[cmap[bx, 0, by] for by in range(2)] for bx in range(2)]
    spot = [[8 * gx + 4 * bx + 2 * lax.rem(gy, 2) + by for by in range(2)] for bx in range(2)]
    packed = jnp.zeros((8, NZ), jnp.int32)
    for bx in range(2):
        for by in range(2):
            packed = jnp.where(sub == 2 * bx + by, nodes[bx][by], packed)
    packed = packed.astype(F32)
    started = []

    def remote(src, dst, ss, rs, peer):
        copy = pltpu.make_async_remote_copy(
            src_ref=src, dst_ref=dst, send_sem=ss, recv_sem=rs, device_id=peer, device_id_type=MESH)
        copy.start()
        started.append(copy)
        return copy

    loads[0].wait()
    loads[1].wait()

    def masked(r, carry):
        ext[0, r + 4, pl.ds(0, T)] = ext[0, r + 4, pl.ds(0, T)] * mask[r].astype(F32)
        return carry

    lax.fori_loop(0, T, masked, 0, unroll=4)
    loads[2].wait()
    cond_f, guess_f, right_f = (view(ext.at[a]) for a in range(3))
    fields = (cond_f, guess_f)

    def column(ref, y):
        return ref[pl.ds(flat_of(0, y), T, stride=STRIDE)]

    def row(ref, x):
        return ref[pl.ds(flat_of(x, 0), T)]

    def line(ref, s, n):
        at = n if s % 2 == 0 else T - 1 - n
        return row(ref, at) if s < 2 else column(ref, at)

    def put(ref, s, n, value):
        at = T + n if s % 2 == 0 else -1 - n
        if s < 2:
            ref[pl.ds(flat_of(at, 0), T)] = value
        else:
            ref[pl.ds(flat_of(0, at), T, stride=STRIDE)] = value

    for s in range(4):
        for a in range(2):
            a_send[s, a] = line(fields[a], s, 0)
    pl.semaphore_wait(barrier, 8 + 2 * (GROUP - 1))
    ac = [remote(a_send.at[s], a_recv.at[s], a_ss.at[s], a_rs.at[s], sides[s]) for s in (2, 3, 0, 1)]
    ac = [ac[2], ac[3], ac[0], ac[1]]
    loads[3].wait()
    bc = [None] * 4
    for s in (2, 3, 0, 1):
        for i in range(2):
            for a in range(2):
                b_send[s, pl.ds(T * (2 * a + i), T)] = line(fields[a], s, 1 + i)
            b_send[s, pl.ds(T * (4 + i), T)] = line(right_f, s, i)
        b_send[s, pl.ds(T * 6, 8)] = packed
        bc[s] = remote(b_send.at[s], b_recv.at[s], b_ss.at[s], b_rs.at[s], sides[s])
    kc = []
    for q in range(4):
        sx, sy = q // 2, q % 2
        x3, y3 = (0, T - 3)[sx], (0, T - 3)[sy]
        x2, y2 = (0, T - 2)[sx], (0, T - 2)[sy]
        for a in range(2):
            for i in range(3):
                k_send[q, pl.ds(9 * a + 3 * i, 3)] = fields[a][pl.ds(flat_of(x3 + i, y3), 3)]
        k_send[q, pl.ds(22, 2)] = jnp.zeros((2, NZ), F32)
        for i in range(2):
            k_send[q, pl.ds(18 + 2 * i, 2)] = right_f[pl.ds(flat_of(x2 + i, y2), 2)]
        kc.append(remote(k_send.at[q], k_recv.at[q], k_ss.at[q], k_rs.at[q], corners[q]))

    def cells(bx):
        def add(r, carry):
            acc, kd = carry
            at = pl.ds(pl.multiple_of((4 + BLK * bx + r) * STRIDE, 8), T)
            q = screen + jnp.maximum(0.0, 1.0 - 2.0 * cond_f[at])
            return acc + (right_f[at] - q * guess_f[at]), kd + q
        zero = jnp.zeros((T, NZ), F32)
        return lax.fori_loop(0, BLK, add, (zero, zero), unroll=4)

    def halves(v):
        return [v[:BLK], v[BLK:]]

    def face(c0, g0, c1, g1):
        w = jnp.minimum(c0, c1)
        return halves(w * (g0 - g1)), halves(w)

    sums, k_cell = [], []
    for bx in range(2):
        acc, kd = cells(bx)
        sums.append(halves(acc))
        k_cell.append(halves(kd))
    mid_x, mid_xw = face(row(cond_f, 15), row(guess_f, 15), row(cond_f, 16), row(guess_f, 16))
    mid_y, mid_yw = face(column(cond_f, 15), column(guess_f, 15), column(cond_f, 16), column(guess_f, 16))
    for i in range(2):
        sums[0][i] -= mid_x[i]
        sums[1][i] += mid_x[i]
        sums[i][0] -= mid_y[i]
        sums[i][1] += mid_y[i]

    def clear(ref, start, n):
        ref[pl.ds(start, n)] = jnp.zeros((n, NZ), F32)

    def clear_column(ref, x, y, n):
        ref[pl.ds(flat_of(x, y), n, stride=STRIDE)] = jnp.zeros((n, NZ), F32)

    for s in range(4):
        ac[s].wait_recv()
        for a in range(2):
            put(fields[a], s, 0, a_recv[s, a])

    @pl.when(gx == 0)
    def _():
        clear(cond_f, flat_of(-1, 0), T)

    @pl.when(gx == n_gx - 1)
    def _():
        clear(cond_f, flat_of(T, 0), T)

    @pl.when(gy == 0)
    def _():
        clear_column(cond_f, 0, -1, T)

    @pl.when(gy == n_gy - 1)
    def _():
        clear_column(cond_f, 0, T, T)

    edge_x = [face(row(cond_f, x), row(guess_f, x), row(cond_f, n), row(guess_f, n)) for x, n in ((0, -1), (T - 1, T))]
    edge_y = [face(column(cond_f, y), column(guess_f, y), column(cond_f, n), column(guess_f, n))
              for y, n in ((0, -1), (T - 1, T))]

    def totals(parts):
        found = []
        for base in range(0, len(parts), 8):
            group = parts[base:base + 8]
            stack = jnp.zeros((8, NZ), F32)
            for i, value in enumerate(group):
                stack = jnp.where(sub == i, jnp.sum(value, axis=0, keepdims=True), stack)
            stack = jnp.sum(stack, axis=1, keepdims=True)
            found += [stack[i:i + 1] for i in range(len(group))]
        return found

    blocks = [(bx, by) for bx in range(2) for by in range(2)]
    k_east = [mid_xw, edge_x[1][1]]
    k_north = [[mid_yw[bx], edge_y[1][1][bx]] for bx in range(2)]
    found = totals(
        [sums[bx][by] - edge_x[bx][0][by] - edge_y[by][0][bx] for bx, by in blocks]
        + [k_cell[bx][by] for bx, by in blocks]
        + [k_east[bx][by] for bx, by in blocks]
        + [k_north[bx][by] for bx, by in blocks])
    vec = jnp.zeros((8, NZ), F32)
    table = jnp.zeros((8, NZ), F32)
    for i, (bx, by) in enumerate(blocks):
        vec = vec + jnp.where(node_of == nodes[bx][by], found[i], 0.0)
        here = lane == spot[bx][by]
        table = jnp.where(here & (sub == 0), packed[i:i + 1], table)
        for q in range(1, 4):
            table = jnp.where(here & (sub == q), found[4 * q + i], table)

    def send_group(stage, value0, value1, peer_of, order):
        part[stage, 0] = value0
        part[stage, 1] = value1
        for k in order:
            pltpu.make_async_remote_copy(
                src_ref=part.at[stage], dst_ref=recv.at[stage, GROUP - 1 - k], send_sem=g_ss.at[stage],
                recv_sem=g_rs.at[stage], device_id=peer_of(k), device_id_type=MESH).start()

    def recv_group(stage):
        pltpu.make_async_copy(recv.at[stage], recv.at[stage], g_rs.at[stage]).wait()

    def relay(stage):
        recv_group(stage)
        both = part[stage] + jnp.sum(recv[stage], axis=0)
        send_group(stage + 1, both[0], both[1], far_peer, far_order)

    def collect(stage, table_out):
        recv_group(stage)
        table_out[pl.ds(0, GROUP - 1)] = recv[stage, :, 1]
        table_out[GROUP - 1] = part[stage, 1]
        return part[stage, 0] + jnp.sum(recv[stage, :, 0], axis=0)

    send_group(0, vec, table, near_peer, near_order)

    w_east_f, w_north_f, w_above_f, diag_f, dinv_f, first_f, e_a_f, e_b_f, d_f = (
        view(ref) for ref in (w_east, w_north, w_above, diag, dinv, first, e_a, e_b, d_ext))

    def prepare(f, n):
        at = pl.ds(f, n)
        c = cond_f[at]
        g = guess_f[at]
        we = jnp.minimum(c, cond_f[pl.ds(f + STRIDE, n)])
        ww = jnp.minimum(c, cond_f[pl.ds(f - STRIDE, n)])
        wn = jnp.minimum(c, cond_f[pl.ds(f + 1, n)])
        ws = jnp.minimum(c, cond_f[pl.ds(f - 1, n)])
        top = lax.broadcasted_iota(jnp.int32, (n, NZ), 1) == NZ - 1
        wa = jnp.where(top, 0.0, jnp.minimum(c, up(c)))
        w_east_f[at] = we
        w_north_f[at] = wn
        w_above_f[at] = wa
        dg = screen + jnp.maximum(0.0, 1.0 - 2.0 * c) + ww + we + ws + wn + down(wa) + wa
        diag_f[at] = dg
        total = ww * guess_f[pl.ds(f - STRIDE, n)] + we * guess_f[pl.ds(f + STRIDE, n)]
        total = total + ws * guess_f[pl.ds(f - 1, n)] + wn * guess_f[pl.ds(f + 1, n)]
        total = total + down(wa * g) + wa * up(g)
        r = right_f[at] - dg * g + total
        di = relax / dg
        dinv_f[at] = di
        first_f[at] = di * r
        return r

    def own_rows(x, carry):
        resid_out[x] = prepare(pl.multiple_of((x + 4) * STRIDE, 8), T)
        return carry

    lax.fori_loop(0, T, own_rows, 0, unroll=4)

    for s in (2, 3, 0, 1):
        bc[s].wait_recv()
        for i in range(2):
            for a in range(2):
                put(fields[a], s, 1 + i, b_recv[s, pl.ds(T * (2 * a + i), T)])
            put(right_f, s, i, b_recv[s, pl.ds(T * (4 + i), T)])
    for q in range(4):
        kc[q].wait_recv()
        sx, sy = q // 2, q % 2
        x3, y3 = (T, -3)[sx], (T, -3)[sy]
        x2, y2 = (T, -2)[sx], (T, -2)[sy]
        for a in range(2):
            for i in range(3):
                fields[a][pl.ds(flat_of(x3 + i, y3), 3)] = k_recv[q, pl.ds(9 * a + 3 * i, 3)]
        for i in range(2):
            right_f[pl.ds(flat_of(x2 + i, y2), 2)] = k_recv[q, pl.ds(18 + 2 * i, 2)]

    @pl.when(gx == 0)
    def _():
        clear(cond_f, flat_of(-3, -4), 3 * STRIDE)

    @pl.when(gx == n_gx - 1)
    def _():
        clear(cond_f, flat_of(T, -4), 3 * STRIDE)

    @pl.when(gy == 0)
    def _():
        for y in (-3, -2, -1):
            clear_column(cond_f, -3, y, T + 6)

    @pl.when(gy == n_gy - 1)
    def _():
        for y in (T, T + 1, T + 2):
            clear_column(cond_f, -3, y, T + 6)

    for x in (-2, -1, T, T + 1):
        prepare(flat_of(x, 0), T)

    def pads(x, carry):
        prepare(pl.multiple_of((x + 1) * STRIDE + T, 8), 8)
        return carry

    lax.fori_loop(0, 37, pads, 0, unroll=4)
    for ref in (dinv_f, first_f):
        clear(ref, flat_of(-3, 32), 6)
        for x in range(-2, 33):
            clear(ref, flat_of(x, 34), 4)
        last = flat_of(33, 34)
        clear(ref, last, LO + CHUNK * STEPS - last)
    for ref in (w_east_f, w_north_f, w_above_f):
        clear(ref, flat_of(34, 0), LO + CHUNK * STEPS - flat_of(34, 0))

    @pl.when(gx == 0)
    def _():
        clear(first_f, flat_of(-2, -4), 2 * STRIDE)

    @pl.when(gx == n_gx - 1)
    def _():
        clear(first_f, flat_of(T, -4), 2 * STRIDE)

    @pl.when(gy == 0)
    def _():
        for y in (-2, -1):
            clear_column(first_f, -2, y, T + 4)

    @pl.when(gy == n_gy - 1)
    def _():
        for y in (T, T + 1):
            clear_column(first_f, -2, y, T + 4)

    def around(ref, f, n):
        at = pl.ds(f, n)
        v = ref[at]
        wa = w_above_f[at]
        total = w_east_f[at] * ref[pl.ds(f + STRIDE, n)]
        total = total + w_east_f[pl.ds(f - STRIDE, n)] * ref[pl.ds(f - STRIDE, n)]
        total = total + w_north_f[at] * ref[pl.ds(f + 1, n)]
        total = total + w_north_f[pl.ds(f - 1, n)] * ref[pl.ds(f - 1, n)]
        return total + wa * up(v) + down(wa * v), v

    def relaxed(src, dst, f, n):
        at = pl.ds(f, n)
        total, v = around(src, f, n)
        dst[at] = (1.0 - relax) * v + first_f[at] + dinv_f[at] * total

    def sweep(src, dst):
        def step(i, carry):
            relaxed(src, dst, pl.multiple_of(LO + i * CHUNK, 8), CHUNK)
            return carry
        lax.fori_loop(0, STEPS, step, 0)

    sweep(first_f, e_a_f)
    relay(0)
    sweep(e_a_f, e_b_f)

    def last_sweep(x, carry):
        relaxed(e_b_f, e_a_f, pl.multiple_of((x + 4) * STRIDE, 8), T)
        return carry

    lax.fori_loop(0, T, last_sweep, 0, unroll=4)
    lc = []
    for s in range(4):
        l_send[s] = line(e_a_f, s, 0)
        lc.append(remote(l_send.at[s], l_recv.at[s], l_ss.at[s], l_rs.at[s], sides[s]))

    coarse_resid = collect(1, near_out)
    coarse_out[1] = coarse_resid
    loads[4].wait()
    acc = jnp.zeros((4, NZ), F32)
    for k in range(8):
        acc = acc + inverse[:, pl.ds(NZ * k, NZ)] * coarse_resid[k:k + 1]
    acc = jnp.sum(acc, axis=1, keepdims=True)
    vec = jnp.zeros((8, NZ), F32)
    base = (gx * n_gy + gy) * 4
    for i in range(4):
        vec = vec + jnp.where(node_of == base + i, acc[i:i + 1], 0.0)

    for s in range(4):
        lc[s].wait_recv()
        put(e_a_f, s, 0, l_recv[s])

    def products(bx):
        def add(r, carry):
            al, lal, rl = carry
            x = BLK * bx + r
            f = pl.multiple_of((x + 4) * STRIDE, 8)
            total, v = around(e_a_f, f, T)
            im = diag_f[pl.ds(f, T)] * v - total
            return al + im, lal + v * im, rl + v * resid_out[x]
        zero = jnp.zeros((T, NZ), F32)
        return [halves(v) for v in lax.fori_loop(0, BLK, add, (zero, zero, zero), unroll=4)]

    sums = [products(0), products(1)]
    found = totals([sums[bx][q][by] for q in range(3) for bx, by in blocks])
    table = jnp.zeros((8, NZ), F32)
    for i, (bx, by) in enumerate(blocks):
        for q in range(3):
            table = jnp.where((lane == spot[bx][by]) & (sub == q), found[4 * q + i], table)
    send_group(2, vec, table, near_peer, near_order)
    relay(2)
    coarse = collect(3, far_out)
    coarse_out[0] = coarse

    def lookup(node):
        hit = jnp.where(node_of == node, coarse, 0.0)
        return jnp.sum(jnp.sum(hit, axis=0, keepdims=True), axis=1, keepdims=True)

    high = lax.broadcasted_iota(jnp.int32, (T, NZ), 0) >= BLK

    def spread(lower, upper):
        return jnp.where(high, upper, lower)

    for bx in range(2):
        mine = spread(lookup(nodes[bx][0]), lookup(nodes[bx][1]))

        def place(r, carry):
            x = BLK * bx + r
            v = e_a[4 + x, pl.ds(0, T)] + mine
            d_ext[4 + x, pl.ds(0, T)] = v
            d_out[x] = v
            return carry

        lax.fori_loop(0, BLK, place, 0, unroll=4)
    pairs = ((0, 1), (2, 3), (0, 2), (1, 3))
    for s in range(4):
        ids = b_recv[s, pl.ds(T * 6, 8)].astype(jnp.int32)
        put(d_f, s, 0, spread(*(lookup(ids[p:p + 1]) for p in pairs[s])) + l_recv[s])

    def apply(x, carry):
        f = pl.multiple_of((x + 4) * STRIDE, 8)
        total, v = around(d_f, f, T)
        image_out[x] = diag_f[pl.ds(f, T)] * v - total
        return carry

    lax.fori_loop(0, T, apply, 0, unroll=4)
    for copy in started:
        copy.wait_send()
    for stage in range(4):
        pltpu.make_async_copy(recv.at[stage], recv.at[stage], g_ss.at[stage]).wait()


def finish(d, image, resid, coarse, near, far, guess, pressure, residual, guess_v, press_v, resid_v, load_sem, out_sem):
    load = pltpu.make_async_copy(guess, guess_v, load_sem)
    load.start()
    near_f, far_f = near.reshape(GROUP * 8, NZ), far.reshape(GROUP * 8, NZ)

    def pick(ref, q):
        return ref[pl.ds(q, GROUP, stride=8)]

    c = coarse[0]
    node = pick(near_f, 0).astype(jnp.int32)
    at_sub, at_lane = node // NZ, lax.rem(node, NZ)
    block = jnp.zeros((GROUP, NZ), F32)
    for s in range(8):
        line = jnp.broadcast_to(c[s:s + 1], (GROUP, NZ))
        hit = jnp.take_along_axis(line, at_lane, axis=1, mode="promise_in_bounds")
        block = jnp.where(at_sub == s, hit, block)
    east = pltpu.roll(block, NZ - 4, 1)
    lane = lax.broadcasted_iota(jnp.int32, (GROUP, NZ), 1)
    north = jnp.where(lax.rem(lane, 4) == 3, pltpu.roll(pltpu.roll(block, 3, 1), GROUP - 1, 0),
                      pltpu.roll(block, NZ - 1, 1))
    to_east, to_north = block - east, block - north
    numer = pick(far_f, 2)
    denom = (pick(far_f, 1) + 2.0 * block * pick(far_f, 0) + pick(near_f, 1) * block * block
             + pick(near_f, 2) * to_east * to_east + pick(near_f, 3) * to_north * to_north)

    def total(v):
        return jnp.sum(jnp.sum(v, axis=0, keepdims=True), axis=1, keepdims=True)

    step = (total(numer) + total(c * coarse[1])) / total(denom)
    load.wait()
    copies = []
    for part in range(4):
        rows = pl.ds(8 * part, 8)
        press_v[rows] = guess_v[rows] + step * d[rows]
        resid_v[rows] = resid[rows] - step * image[rows]
        copies.append(pltpu.make_async_copy(press_v.at[rows], pressure.at[rows], out_sem.at[2 * part]))
        copies.append(pltpu.make_async_copy(resid_v.at[rows], residual.at[rows], out_sem.at[2 * part + 1]))
        copies[-2].start()
        copies[-1].start()
    for copy in copies:
        copy.wait()


def body(right_side, guess, conductivity, wet_mask, coarse_map, coarse_inverse):
    tile = jax.ShapeDtypeStruct((T, T, NZ), F32)
    table = jax.ShapeDtypeStruct((GROUP, 8, NZ), F32)
    hbm = pl.BlockSpec(memory_space=pltpu.HBM)
    vmem = pl.BlockSpec(memory_space=pltpu.VMEM)
    field = pltpu.VMEM((ROWS, STRIDE, NZ), F32)
    dma = pltpu.SemaphoreType.DMA
    state = pl.pallas_call(
        kernel,
        out_shape=(tile, tile, tile, jax.ShapeDtypeStruct((2, 8, NZ), F32), table, table),
        in_specs=[pl.BlockSpec(memory_space=pltpu.SMEM)] + [hbm] * 5,
        out_specs=(vmem,) * 6,
        scratch_shapes=[
            pltpu.VMEM((3, ROWS, STRIDE, NZ), F32), pltpu.VMEM((T, T, NZ), jnp.int32),
        ] + [field] * 9 + [
            pltpu.VMEM((4, NODES), F32),
            pltpu.VMEM((4, 2, T, NZ), F32), pltpu.VMEM((4, 2, T, NZ), F32),
            pltpu.VMEM((4, 6 * T + 8, NZ), F32), pltpu.VMEM((4, 6 * T + 8, NZ), F32),
            pltpu.VMEM((4, 24, NZ), F32), pltpu.VMEM((4, 24, NZ), F32),
            pltpu.VMEM((4, T, NZ), F32), pltpu.VMEM((4, T, NZ), F32),
            pltpu.VMEM((4, 2, 8, NZ), F32), pltpu.VMEM((4, GROUP - 1, 2, 8, NZ), F32),
            dma((5,)),
        ] + [dma((4,))] * 10,
        compiler_params=pltpu.CompilerParams(
            collective_id=0, has_side_effects=True, vmem_limit_bytes=40 * 1024 * 1024),
    )(*(pltpu.with_memory_space_constraint(array, pltpu.HBM) for array in (
        coarse_map.transpose(0, 2, 1), coarse_inverse, right_side, guess, conductivity, wet_mask)))
    return pl.pallas_call(
        finish,
        out_shape=(tile, tile),
        in_specs=[vmem] * 6 + [hbm],
        out_specs=(hbm, hbm),
        scratch_shapes=[pltpu.VMEM((T, T, NZ), F32)] * 3 + [dma, dma((8,))],
        compiler_params=pltpu.CompilerParams(vmem_limit_bytes=16 * 1024 * 1024),
    )(*state, pltpu.with_memory_space_constraint(guess, pltpu.HBM))


def solution(mesh):
    grid = P("gx", "gy", None)
    in_specs = (grid, grid, grid, grid, grid, P(("gx", "gy"), None))
    return jax.shard_map(body, mesh=mesh, in_specs=in_specs, out_specs=(grid, grid), check_vma=False)
```

time: 59.9 us -> 43.6 us (0.73)
  Pallas kernels: 50.8 us -> 42.8 us
  local copies, waits for them, and re-layouts: 6.24 us -> 0 us
  other arithmetic: 1.88 us -> 0 us
    pallas_call x1, Pallas kernels: 50.8 us -> 40.6 us  [body(): pl.pallas_call(kernel, out_shape=(tile, tile, tile, jax.ShapeDtypeStruct(...]
    unnamed x11 -> x0, local copies, waits for them, and re-layouts: 5.65 us -> none
    pallas_call x0 -> x1, Pallas kernels: none -> 2.19 us  [body(): pl.pallas_call(finish, out_shape=(tile, tile), in_specs=[vmem] * 6 + [hbm...]
    sub x1 -> x0, other arithmetic: 1.88 us -> none  [body(): return (guess + step * d, resid - step * image)]
where the time goes in v2:
time: 43.6 us; the launch traced here: 43.4 us
  Pallas kernels  42.8 us (98%)
  between operations  0.64 us (1%)
    pallas_call x1, Pallas kernels, body(): pl.pallas_call(kernel, out_shape=(tile, tile, tile, jax.ShapeDtypeStruct(...  40.6 us
    pallas_call x1, Pallas kernels, body(): pl.pallas_call(finish, out_shape=(tile, tile), in_specs=[vmem] * 6 + [hbm...  2.19 us

profile of v2, /device:TPU:1, one launch (start us, length us, event | category | flops | bytes accessed | tf_op | source)
XLA Modules:
  0.0 43.4 jit_solution(11816480275547273142)
XLA Ops:
  0.6 40.6 %shard_map.77 = (f32[32,32,128]{2,1,0:T(8,128)S(1)}, f32[32,32,128]{2,1,0:T(8,128)S(1)}, f32[32,32,128]{2,1,0:T(8,128)S(1)}, f32[2,8,128]{2,1,0:T(8,128)S(1)}, f...) custom-call(s32[2,1,2]{2,1,0:T(1,128)} %bitcast.3, f32[4,1024]{1,0:T(4,128)} %cinv.1, f32[32,32,128]{2,1,0:T(8,128)} %right.1, ...), custom_call_target="tpu_custom_call" | custom-call | tf_op jit(solution)/shard_map/pallas_call | solution.py:548
  41.2 2.2 %shard_map.78 = (f32[32,32,128]{2,1,0:T(8,128)}, f32[32,32,128]{2,1,0:T(8,128)}) custom-call(f32[32,32,128]{2,1,0:T(8,128)S(1)} %get-tuple-element.8.d, f32[32,32,128]{2,1,0:T(8,128)S(1)} %get-tuple-element.9.image, f32[32,32,128]{2,1,0:T(8,128)S(1)} %get-tuple-element.10.resid, f32[2,8,128]{2,1,0:T(8,128)S(1)} %get-tuple-element.11.coarse, ...), custom_call_target="tpu_custom_call" | custom-call | tf_op jit(solution)/shard_map/pallas_call | solution.py:568

commit v3 on v2

--- a/solution.py
+++ b/solution.py
@@ -38,8 +38,8 @@
 
 def kernel(
     cmap, cinv, right, guess, conductivity, wet,
-    d_out, image_out, resid_out, coarse_out, near_out, far_out,
-    ext, mask, w_east, w_north, w_above, diag, dinv, first, e_a, e_b, d_ext, inverse,
+    l_out, image_out, resid_out, q_out, faces_out, coarse_out, near_out, far_out,
+    ext, mask, w_east, w_north, w_above, diag, dinv, first, e_a, e_b, e_c, inverse,
     a_send, a_recv, b_send, b_recv, k_send, k_recv, l_send, l_recv,
     part, recv,
     load_sem, a_ss, a_rs, b_ss, b_rs, k_ss, k_rs, l_ss, l_rs, g_ss, g_rs,
@@ -66,10 +66,6 @@
     near_order = (8, 7, 9, 6, 10, 5, 11, 4, 12, 3, 13, 2, 14, 1, 15)
     far_order = (8, 7, 9, 6, 10, 5, 11, 4, 12, 3, 13, 2, 14, 1, 15)
 
-    barrier = pltpu.get_barrier_semaphore()
-    for peer in [far_peer(k) for k in far_order] + [near_peer(k) for k in near_order] + corners + list(sides):
-        pl.semaphore_signal(barrier, inc=1, device_id=peer, device_id_type=MESH)
-
     own = (pl.ds(4, T), pl.ds(0, T))
     loads = [
         pltpu.make_async_copy(conductivity, ext.at[(0,) + own], load_sem.at[0]),
@@ -81,17 +77,25 @@
     for copy in loads:
         copy.start()
 
+    barrier = pltpu.get_barrier_semaphore()
+    for peer in [far_peer(k) for k in far_order] + [near_peer(k) for k in near_order] + corners + list(sides):
+        pl.semaphore_signal(barrier, inc=1, device_id=peer, device_id_type=MESH)
+
     pad = jnp.zeros((8, NZ), F32)
     wide = jnp.zeros((STRIDE, NZ), F32)
-    for a in range(3):
+    for ref in [ext.at[a] for a in range(3)] + [w_east, w_north, w_above, dinv, first]:
         for r in (0, 1, 2, 3, 36, 37, 38, 39):
-            ext[a, r] = wide
+            ref[r] = wide
         for r in range(4, 36):
-            ext[a, r, pl.ds(32, 8)] = pad
-    for ref in (w_east, w_north, first, e_a, e_b):
+            ref[r, pl.ds(32, 8)] = pad
+    for ref in (e_a, e_b):
         view(ref)[pl.ds(0, LO)] = jnp.zeros((LO, NZ), F32)
         view(ref)[pl.ds(LO + CHUNK * STEPS, FLAT - LO - CHUNK * STEPS)] = jnp.zeros(
             (FLAT - LO - CHUNK * STEPS, NZ), F32)
+    for r in (3, 36):
+        e_c[r] = wide
+    for r in range(4, 36):
+        e_c[r, pl.ds(32, 8)] = pad
 
     sub = lax.broadcasted_iota(jnp.int32, (8, NZ), 0)
     lane = lax.broadcasted_iota(jnp.int32, (8, NZ), 1)
@@ -169,11 +173,47 @@
             k_send[q, pl.ds(18 + 2 * i, 2)] = right_f[pl.ds(flat_of(x2 + i, y2), 2)]
         kc.append(remote(k_send.at[q], k_recv.at[q], k_ss.at[q], k_rs.at[q], corners[q]))
 
+    w_east_f, w_north_f, w_above_f, diag_f, dinv_f, first_f, e_a_f, e_b_f, e_c_f = (
+        view(ref) for ref in (w_east, w_north, w_above, diag, dinv, first, e_a, e_b, e_c))
+    resid_f, image_f = (ref.reshape(T * T, NZ) for ref in (resid_out, image_out))
+
+    def prepare(f, n, stride):
+        def at(shift=0):
+            return pl.ds(f + shift, n) if stride == 1 else pl.ds(f + shift, n, stride=stride)
+        c = cond_f[at()]
+        g = guess_f[at()]
+        we = jnp.minimum(c, cond_f[at(STRIDE)])
+        ww = jnp.minimum(c, cond_f[at(-STRIDE)])
+        wn = jnp.minimum(c, cond_f[at(1)])
+        ws = jnp.minimum(c, cond_f[at(-1)])
+        top = lax.broadcasted_iota(jnp.int32, (n, NZ), 1) == NZ - 1
+        wa = jnp.where(top, 0.0, jnp.minimum(c, up(c)))
+        w_east_f[at()] = we
+        w_north_f[at()] = wn
+        w_above_f[at()] = wa
+        dg = screen + jnp.maximum(0.0, 1.0 - 2.0 * c) + ww + we + ws + wn + down(wa) + wa
+        diag_f[at()] = dg
+        total = ww * guess_f[at(-STRIDE)] + we * guess_f[at(STRIDE)]
+        total = total + ws * guess_f[at(-1)] + wn * guess_f[at(1)]
+        total = total + down(wa * g) + wa * up(g)
+        r = right_f[at()] - dg * g + total
+        di = relax / dg
+        dinv_f[at()] = di
+        first_f[at()] = di * r
+        return r
+
+    def own_rows(x, carry):
+        resid_out[x] = prepare(pl.multiple_of((x + 4) * STRIDE, 8), T, 1)
+        return carry
+
+    lax.fori_loop(0, T, own_rows, 0, unroll=4)
+
     def cells(bx):
         def add(r, carry):
             acc, kd = carry
             at = pl.ds(pl.multiple_of((4 + BLK * bx + r) * STRIDE, 8), T)
             q = screen + jnp.maximum(0.0, 1.0 - 2.0 * cond_f[at])
+            q_out[BLK * bx + r] = q
             return acc + (right_f[at] - q * guess_f[at]), kd + q
         zero = jnp.zeros((T, NZ), F32)
         return lax.fori_loop(0, BLK, add, (zero, zero), unroll=4)
@@ -183,7 +223,7 @@
 
     def face(c0, g0, c1, g1):
         w = jnp.minimum(c0, c1)
-        return halves(w * (g0 - g1)), halves(w)
+        return halves(w * (g0 - g1)), w
 
     sums, k_cell = [], []
     for bx in range(2):
@@ -241,8 +281,11 @@
         return found
 
     blocks = [(bx, by) for bx in range(2) for by in range(2)]
-    k_east = [mid_xw, edge_x[1][1]]
-    k_north = [[mid_yw[bx], edge_y[1][1][bx]] for bx in range(2)]
+    w_side = [edge_x[0][1], edge_x[1][1], edge_y[0][1], edge_y[1][1]]
+    for i, w in enumerate((w_side[0], mid_xw, w_side[1], w_side[2], mid_yw, w_side[3])):
+        faces_out[i] = w
+    k_east = [halves(mid_xw), halves(w_side[1])]
+    k_north = [[halves(mid_yw)[bx], halves(w_side[3])[bx]] for bx in range(2)]
     found = totals(
         [sums[bx][by] - edge_x[bx][0][by] - edge_y[by][0][bx] for bx, by in blocks]
         + [k_cell[bx][by] for bx, by in blocks]
@@ -268,6 +311,9 @@
     def recv_group(stage):
         pltpu.make_async_copy(recv.at[stage], recv.at[stage], g_rs.at[stage]).wait()
 
+    def sent(stage):
+        pltpu.make_async_copy(recv.at[stage], recv.at[stage], g_ss.at[stage]).wait()
+
     def relay(stage):
         recv_group(stage)
         both = part[stage] + jnp.sum(recv[stage], axis=0)
@@ -281,38 +327,10 @@
 
     send_group(0, vec, table, near_peer, near_order)
 
-    w_east_f, w_north_f, w_above_f, diag_f, dinv_f, first_f, e_a_f, e_b_f, d_f = (
-        view(ref) for ref in (w_east, w_north, w_above, diag, dinv, first, e_a, e_b, d_ext))
-
-    def prepare(f, n):
-        at = pl.ds(f, n)
-        c = cond_f[at]
-        g = guess_f[at]
-        we = jnp.minimum(c, cond_f[pl.ds(f + STRIDE, n)])
-        ww = jnp.minimum(c, cond_f[pl.ds(f - STRIDE, n)])
-        wn = jnp.minimum(c, cond_f[pl.ds(f + 1, n)])
-        ws = jnp.minimum(c, cond_f[pl.ds(f - 1, n)])
-        top = lax.broadcasted_iota(jnp.int32, (n, NZ), 1) == NZ - 1
-        wa = jnp.where(top, 0.0, jnp.minimum(c, up(c)))
-        w_east_f[at] = we
-        w_north_f[at] = wn
-        w_above_f[at] = wa
-        dg = screen + jnp.maximum(0.0, 1.0 - 2.0 * c) + ww + we + ws + wn + down(wa) + wa
-        diag_f[at] = dg
-        total = ww * guess_f[pl.ds(f - STRIDE, n)] + we * guess_f[pl.ds(f + STRIDE, n)]
-        total = total + ws * guess_f[pl.ds(f - 1, n)] + wn * guess_f[pl.ds(f + 1, n)]
-        total = total + down(wa * g) + wa * up(g)
-        r = right_f[at] - dg * g + total
-        di = relax / dg
-        dinv_f[at] = di
-        first_f[at] = di * r
-        return r
-
-    def own_rows(x, carry):
-        resid_out[x] = prepare(pl.multiple_of((x + 4) * STRIDE, 8), T)
-        return carry
-
-    lax.fori_loop(0, T, own_rows, 0, unroll=4)
+    for x in (0, T - 1):
+        resid_f[pl.ds(T * x, T)] = prepare(flat_of(x, 0), T, 1)
+    for y in (0, T - 1):
+        resid_f[pl.ds(y, T, stride=T)] = prepare(flat_of(0, y), T, STRIDE)
 
     for s in (2, 3, 0, 1):
         bc[s].wait_recv()
@@ -350,21 +368,9 @@
             clear_column(cond_f, -3, y, T + 6)
 
     for x in (-2, -1, T, T + 1):
-        prepare(flat_of(x, 0), T)
-
-    def pads(x, carry):
-        prepare(pl.multiple_of((x + 1) * STRIDE + T, 8), 8)
-        return carry
-
-    lax.fori_loop(0, 37, pads, 0, unroll=4)
-    for ref in (dinv_f, first_f):
-        clear(ref, flat_of(-3, 32), 6)
-        for x in range(-2, 33):
-            clear(ref, flat_of(x, 34), 4)
-        last = flat_of(33, 34)
-        clear(ref, last, LO + CHUNK * STEPS - last)
-    for ref in (w_east_f, w_north_f, w_above_f):
-        clear(ref, flat_of(34, 0), LO + CHUNK * STEPS - flat_of(34, 0))
+        prepare(flat_of(x, 0), T, 1)
+    for y in (-2, -1, T, T + 1):
+        prepare(flat_of(-2, y), T + 4, STRIDE)
 
     @pl.when(gx == 0)
     def _():
@@ -410,14 +416,29 @@
     sweep(e_a_f, e_b_f)
 
     def last_sweep(x, carry):
-        relaxed(e_b_f, e_a_f, pl.multiple_of((x + 4) * STRIDE, 8), T)
+        relaxed(e_b_f, e_c_f, pl.multiple_of((x + 4) * STRIDE, 8), T)
         return carry
 
     lax.fori_loop(0, T, last_sweep, 0, unroll=4)
     lc = []
     for s in range(4):
-        l_send[s] = line(e_a_f, s, 0)
+        l_send[s] = line(e_c_f, s, 0)
         lc.append(remote(l_send.at[s], l_recv.at[s], l_ss.at[s], l_rs.at[s], sides[s]))
+
+    def products(bx):
+        def add(r, carry):
+            al, lal, rl = carry
+            x = BLK * bx + r
+            f = pl.multiple_of((x + 4) * STRIDE, 8)
+            total, v = around(e_c_f, f, T)
+            im = diag_f[pl.ds(f, T)] * v - total
+            image_out[x] = im
+            l_out[x] = v
+            return al + im, lal + v * im, rl + v * resid_out[x]
+        zero = jnp.zeros((T, NZ), F32)
+        return [halves(v) for v in lax.fori_loop(0, BLK, add, (zero, zero, zero), unroll=4)]
+
+    sums = [products(0), products(1)]
 
     coarse_resid = collect(1, near_out)
     coarse_out[1] = coarse_resid
@@ -431,22 +452,18 @@
     for i in range(4):
         vec = vec + jnp.where(node_of == base + i, acc[i:i + 1], 0.0)
 
+    for copy in lc:
+        copy.wait_recv()
     for s in range(4):
-        lc[s].wait_recv()
-        put(e_a_f, s, 0, l_recv[s])
-
-    def products(bx):
-        def add(r, carry):
-            al, lal, rl = carry
-            x = BLK * bx + r
-            f = pl.multiple_of((x + 4) * STRIDE, 8)
-            total, v = around(e_a_f, f, T)
-            im = diag_f[pl.ds(f, T)] * v - total
-            return al + im, lal + v * im, rl + v * resid_out[x]
-        zero = jnp.zeros((T, NZ), F32)
-        return [halves(v) for v in lax.fori_loop(0, BLK, add, (zero, zero, zero), unroll=4)]
-
-    sums = [products(0), products(1)]
+        out = w_side[s] * l_recv[s ^ 1]
+        lost = halves(out), halves(out * l_send[s])
+        for i in range(2):
+            bx, by = (s % 2, i) if s < 2 else (i, s % 2)
+            for q in range(2):
+                sums[bx][q][by] -= lost[q][i]
+        at = pl.ds((T - 1) * T * (s % 2), T) if s < 2 else pl.ds((T - 1) * (s % 2), T, stride=T)
+        image_f[at] -= out
+
     found = totals([sums[bx][q][by] for q in range(3) for bx, by in blocks])
     table = jnp.zeros((8, NZ), F32)
     for i, (bx, by) in enumerate(blocks):
@@ -454,54 +471,22 @@
             table = jnp.where((lane == spot[bx][by]) & (sub == q), found[4 * q + i], table)
     send_group(2, vec, table, near_peer, near_order)
     relay(2)
-    coarse = collect(3, far_out)
-    coarse_out[0] = coarse
-
-    def lookup(node):
-        hit = jnp.where(node_of == node, coarse, 0.0)
-        return jnp.sum(jnp.sum(hit, axis=0, keepdims=True), axis=1, keepdims=True)
-
-    high = lax.broadcasted_iota(jnp.int32, (T, NZ), 0) >= BLK
-
-    def spread(lower, upper):
-        return jnp.where(high, upper, lower)
-
-    for bx in range(2):
-        mine = spread(lookup(nodes[bx][0]), lookup(nodes[bx][1]))
-
-        def place(r, carry):
-            x = BLK * bx + r
-            v = e_a[4 + x, pl.ds(0, T)] + mine
-            d_ext[4 + x, pl.ds(0, T)] = v
-            d_out[x] = v
-            return carry
-
-        lax.fori_loop(0, BLK, place, 0, unroll=4)
-    pairs = ((0, 1), (2, 3), (0, 2), (1, 3))
-    for s in range(4):
-        ids = b_recv[s, pl.ds(T * 6, 8)].astype(jnp.int32)
-        put(d_f, s, 0, spread(*(lookup(ids[p:p + 1]) for p in pairs[s])) + l_recv[s])
-
-    def apply(x, carry):
-        f = pl.multiple_of((x + 4) * STRIDE, 8)
-        total, v = around(d_f, f, T)
-        image_out[x] = diag_f[pl.ds(f, T)] * v - total
-        return carry
-
-    lax.fori_loop(0, T, apply, 0, unroll=4)
     for copy in started:
         copy.wait_send()
-    for stage in range(4):
-        pltpu.make_async_copy(recv.at[stage], recv.at[stage], g_ss.at[stage]).wait()
-
-
-def finish(d, image, resid, coarse, near, far, guess, pressure, residual, guess_v, press_v, resid_v, load_sem, out_sem):
+    for stage in range(3):
+        sent(stage)
+    coarse_out[0] = collect(3, far_out)
+    sent(3)
+
+
+def finish(l, image, resid, q, faces, coarse, near, far, guess, pressure, residual, guess_v, press_v, resid_v, load_sem, out_sem):
     load = pltpu.make_async_copy(guess, guess_v, load_sem)
     load.start()
+    gx, gy = lax.axis_index("gx"), lax.axis_index("gy")
     near_f, far_f = near.reshape(GROUP * 8, NZ), far.reshape(GROUP * 8, NZ)
 
-    def pick(ref, q):
-        return ref[pl.ds(q, GROUP, stride=8)]
+    def pick(ref, i):
+        return ref[pl.ds(i, GROUP, stride=8)]
 
     c = coarse[0]
     node = pick(near_f, 0).astype(jnp.int32)
@@ -524,15 +509,48 @@
         return jnp.sum(jnp.sum(v, axis=0, keepdims=True), axis=1, keepdims=True)
 
     step = (total(numer) + total(c * coarse[1])) / total(denom)
+    odd = lax.rem(gy, 2)
+    turn = lax.rem(NZ - 8 * gx - 2 * odd, NZ)
+    block, to_east, to_north = (pltpu.roll(v, turn, 1) for v in (block, to_east, to_north))
+
+    def value(v, slot, at):
+        return v[slot:slot + 1, at % NZ:at % NZ + 1]
+
+    high = lax.broadcasted_iota(jnp.int32, (T, NZ), 0) >= BLK
+
+    def spread(lower, upper):
+        return step * jnp.where(high, upper, lower)
+
+    last = GROUP - 1
+    mine = [spread(value(block, last, 4 * bx), value(block, last, 4 * bx + 1)) for bx in range(2)]
+    flux_x = [faces[i] * spread(value(to_east, last, 4 * (i - 1)), value(to_east, last, 4 * (i - 1) + 1))
+              for i in range(3)]
+    below = [jnp.where(odd == 1, value(to_north, last, 4 * bx - 1), value(to_north, last - 1, 4 * bx + 3))
+             for bx in range(2)]
+    flux_y = [faces[3] * spread(*below)] + [
+        faces[3 + i] * spread(value(to_north, last, i - 1), value(to_north, last, 4 + i - 1)) for i in (1, 2)]
+    flat = resid_v.reshape(T * T, NZ)
     load.wait()
     copies = []
     for part in range(4):
         rows = pl.ds(8 * part, 8)
-        press_v[rows] = guess_v[rows] + step * d[rows]
-        resid_v[rows] = resid[rows] - step * image[rows]
+        add = mine[part // 2]
+        press_v[rows] = guess_v[rows] + step * l[rows] + add
         copies.append(pltpu.make_async_copy(press_v.at[rows], pressure.at[rows], out_sem.at[2 * part]))
+        copies[-1].start()
+        resid_v[rows] = resid[rows] - step * image[rows] - q[rows] * add
+        if part == 0:
+            resid_v[0] += flux_x[0]
+        elif part == 1:
+            resid_v[15] -= flux_x[1]
+        elif part == 2:
+            resid_v[16] += flux_x[1]
+        else:
+            resid_v[31] -= flux_x[2]
+        some = slice(8 * part, 8 * part + 8)
+        for y, i, sign in ((0, 0, 1.0), (15, 1, -1.0), (16, 1, 1.0), (31, 2, -1.0)):
+            flat[pl.ds(8 * part * T + y, 8, stride=T)] += sign * flux_y[i][some]
         copies.append(pltpu.make_async_copy(resid_v.at[rows], residual.at[rows], out_sem.at[2 * part + 1]))
-        copies[-2].start()
         copies[-1].start()
     for copy in copies:
         copy.wait()
@@ -547,9 +565,10 @@
     dma = pltpu.SemaphoreType.DMA
     state = pl.pallas_call(
         kernel,
-        out_shape=(tile, tile, tile, jax.ShapeDtypeStruct((2, 8, NZ), F32), table, table),
+        out_shape=(tile, tile, tile, tile, jax.ShapeDtypeStruct((6, T, NZ), F32),
+                   jax.ShapeDtypeStruct((2, 8, NZ), F32), table, table),
         in_specs=[pl.BlockSpec(memory_space=pltpu.SMEM)] + [hbm] * 5,
-        out_specs=(vmem,) * 6,
+        out_specs=(vmem,) * 8,
         scratch_shapes=[
             pltpu.VMEM((3, ROWS, STRIDE, NZ), F32), pltpu.VMEM((T, T, NZ), jnp.int32),
         ] + [field] * 9 + [
@@ -568,7 +587,7 @@
     return pl.pallas_call(
         finish,
         out_shape=(tile, tile),
-        in_specs=[vmem] * 6 + [hbm],
+        in_specs=[vmem] * 8 + [hbm],
         out_specs=(hbm, hbm),
         scratch_shapes=[pltpu.VMEM((T, T, NZ), F32)] * 3 + [dma, dma((8,))],
         compiler_params=pltpu.CompilerParams(vmem_limit_bytes=16 * 1024 * 1024),

time: 43.6 us -> 42.3 us (0.970)
  Pallas kernels: 42.8 us -> 41.5 us
    pallas_call x2, Pallas kernels: 42.8 us -> 41.5 us  [the longest x1 39.2 us: body(): pl.pallas_call(kernel, out_shape=(tile, tile, tile, tile, jax.ShapeDtypeS...]
where the time goes in v3:
time: 42.3 us; the launch traced here: 42.1 us
  Pallas kernels  41.5 us (98%)
  between operations  0.64 us (2%)
    pallas_call x1, Pallas kernels, body(): pl.pallas_call(kernel, out_shape=(tile, tile, tile, tile, jax.ShapeDtypeS...  39.2 us
    pallas_call x1, Pallas kernels, body(): pl.pallas_call(finish, out_shape=(tile, tile), in_specs=[vmem] * 8 + [hbm...  2.28 us

profile of v3, /device:TPU:1, one launch (start us, length us, event | category | flops | bytes accessed | tf_op | source)
XLA Modules:
  0.0 42.1 jit_solution(18392388784434832682)
XLA Ops:
  0.6 39.2 %shard_map.77 = (f32[32,32,128]{2,1,0:T(8,128)S(1)}, f32[32,32,128]{2,1,0:T(8,128)S(1)}, f32[32,32,128]{2,1,0:T(8,128)S(1)}, f32[32,32,128]{2,1,0:T(8,128)S(1)},...) custom-call(s32[2,1,2]{2,1,0:T(1,128)} %bitcast.3, ...), custom_call_target="tpu_custom_call" | custom-call | tf_op jit(solution)/shard_map/pallas_call | solution.py:566
  39.8 2.3 %shard_map.78 = (f32[32,32,128]{2,1,0:T(8,128)}, f32[32,32,128]{2,1,0:T(8,128)}) custom-call(f32[32,32,128]{2,1,0:T(8,128)S(1)} %get-tuple-element.10.l, f32[32,32,128]{2,1,0:T(8,128)S(1)} %get-tuple-element.11.image, f32[32,32,128]{2,1,0:T(8,128)S(1)} %get-tuple-element.12.resid, f32[32,32,128]{2,1,0:T(8,128)S(1)} %get-tuple-element.13.q, ...), custom_call_target="tpu_custom_call" | custom-call | tf_op jit(solution)/shard_map/pallas_call | solution.py:587

commit v4 on v3

--- a/solution.py
+++ b/solution.py
@@ -14,7 +14,7 @@
 ROWS = 40
 FLAT = ROWS * STRIDE
 NODES = 1024
-GROUP = 16
+PLANE, DEPTH = 32, 8
 screen = 0.02
 relax = 0.8
 LO, CHUNK, STEPS = 72, 112, 13
@@ -38,11 +38,11 @@
 
 def kernel(
     cmap, cinv, right, guess, conductivity, wet,
-    l_out, image_out, resid_out, q_out, faces_out, coarse_out, near_out, far_out,
+    l_out, image_out, resid_out, q_out, faces_out, near_out, far_out,
     ext, mask, w_east, w_north, w_above, diag, dinv, first, e_a, e_b, e_c, inverse,
     a_send, a_recv, b_send, b_recv, k_send, k_recv, l_send, l_recv,
-    part, recv,
-    load_sem, a_ss, a_rs, b_ss, b_rs, k_ss, k_rs, l_ss, l_rs, g_ss, g_rs,
+    p_send, p_recv, z_send, z_recv, t_send, t_recv,
+    load_sem, a_ss, a_rs, b_ss, b_rs, k_ss, k_rs, l_ss, l_rs, p_ss, p_rs, z_ss, z_rs,
 ):
     gx, gy = lax.axis_index("gx"), lax.axis_index("gy")
     n_gx, n_gy = lax.axis_size("gx"), lax.axis_size("gy")
@@ -52,19 +52,22 @@
     north = (gx, lax.rem(gy + 1, n_gy))
     corners = [(px[0], py[1]) for px in (west, east) for py in (south, north)]
     sides = (west, east, south, north)
-    near = gx * 2 + lax.rem(gy, 2)
-    far = gy // 2
-
-    def near_peer(k):
-        j = lax.rem(near + k, GROUP)
-        return (j // 2, far * 2 + lax.rem(j, 2))
-
-    def far_peer(k):
-        j = lax.rem(far + k, GROUP)
-        return (gx, j * 2 + lax.rem(gy, 2))
-
-    near_order = (8, 7, 9, 6, 10, 5, 11, 4, 12, 3, 13, 2, 14, 1, 15)
-    far_order = (8, 7, 9, 6, 10, 5, 11, 4, 12, 3, 13, 2, 14, 1, 15)
+    chip_z, chip_y = gy // 4, lax.rem(gy, 4)
+    chip_x, core = gx // 2, lax.rem(gx, 2)
+
+    offsets = sorted(
+        ((dx, dc, dy) for dx in range(4) for dc in range(2) for dy in range(4) if dx + dc + dy > 0),
+        key=lambda o: (-min(o[0], 4 - o[0]) - min(o[2], 4 - o[2]), -o[1]))
+    planes = (4, 3, 5, 2, 6, 1, 7)
+
+    def plane_peer(o):
+        return (lax.rem(chip_x + o[0], 4) * 2 + lax.rem(core + o[1], 2), chip_z * 4 + lax.rem(chip_y + o[2], 4))
+
+    def plane_slot(o):
+        return offsets.index(((4 - o[0]) % 4, o[1], (4 - o[2]) % 4))
+
+    def depth_peer(k):
+        return (gx, lax.rem(chip_z + k, DEPTH) * 4 + chip_y)
 
     own = (pl.ds(4, T), pl.ds(0, T))
     loads = [
@@ -78,7 +81,7 @@
         copy.start()
 
     barrier = pltpu.get_barrier_semaphore()
-    for peer in [far_peer(k) for k in far_order] + [near_peer(k) for k in near_order] + corners + list(sides):
+    for peer in [depth_peer(k) for k in planes] + [plane_peer(o) for o in offsets] + corners + list(sides):
         pl.semaphore_signal(barrier, inc=1, device_id=peer, device_id_type=MESH)
 
     pad = jnp.zeros((8, NZ), F32)
@@ -101,7 +104,7 @@
     lane = lax.broadcasted_iota(jnp.int32, (8, NZ), 1)
     node_of = sub * NZ + lane
     nodes = [[cmap[bx, 0, by] for by in range(2)] for bx in range(2)]
-    spot = [[8 * gx + 4 * bx + 2 * lax.rem(gy, 2) + by for by in range(2)] for bx in range(2)]
+    spot = [[16 * gx + 8 * bx + 2 * chip_y + by for by in range(2)] for bx in range(2)]
     packed = jnp.zeros((8, NZ), jnp.int32)
     for bx in range(2):
         for by in range(2):
@@ -123,7 +126,7 @@
         ext[0, r + 4, pl.ds(0, T)] = ext[0, r + 4, pl.ds(0, T)] * mask[r].astype(F32)
         return carry
 
-    lax.fori_loop(0, T, masked, 0, unroll=4)
+    lax.fori_loop(0, T, masked, 0, unroll=16)
     loads[2].wait()
     cond_f, guess_f, right_f = (view(ext.at[a]) for a in range(3))
     fields = (cond_f, guess_f)
@@ -148,7 +151,7 @@
     for s in range(4):
         for a in range(2):
             a_send[s, a] = line(fields[a], s, 0)
-    pl.semaphore_wait(barrier, 8 + 2 * (GROUP - 1))
+    pl.semaphore_wait(barrier, 8 + len(planes) + len(offsets))
     ac = [remote(a_send.at[s], a_recv.at[s], a_ss.at[s], a_rs.at[s], sides[s]) for s in (2, 3, 0, 1)]
     ac = [ac[2], ac[3], ac[0], ac[1]]
     loads[3].wait()
@@ -206,7 +209,7 @@
         resid_out[x] = prepare(pl.multiple_of((x + 4) * STRIDE, 8), T, 1)
         return carry
 
-    lax.fori_loop(0, T, own_rows, 0, unroll=4)
+    lax.fori_loop(0, T, own_rows, 0, unroll=16)
 
     def cells(bx):
         def add(r, carry):
@@ -216,7 +219,7 @@
             q_out[BLK * bx + r] = q
             return acc + (right_f[at] - q * guess_f[at]), kd + q
         zero = jnp.zeros((T, NZ), F32)
-        return lax.fori_loop(0, BLK, add, (zero, zero), unroll=4)
+        return lax.fori_loop(0, BLK, add, (zero, zero), unroll=16)
 
     def halves(v):
         return [v[:BLK], v[BLK:]]
@@ -291,41 +294,34 @@
         + [k_cell[bx][by] for bx, by in blocks]
         + [k_east[bx][by] for bx, by in blocks]
         + [k_north[bx][by] for bx, by in blocks])
-    vec = jnp.zeros((8, NZ), F32)
     table = jnp.zeros((8, NZ), F32)
     for i, (bx, by) in enumerate(blocks):
-        vec = vec + jnp.where(node_of == nodes[bx][by], found[i], 0.0)
         here = lane == spot[bx][by]
         table = jnp.where(here & (sub == 0), packed[i:i + 1], table)
-        for q in range(1, 4):
-            table = jnp.where(here & (sub == q), found[4 * q + i], table)
-
-    def send_group(stage, value0, value1, peer_of, order):
-        part[stage, 0] = value0
-        part[stage, 1] = value1
-        for k in order:
+        for q in range(4):
+            table = jnp.where(here & (sub == (4, 1, 2, 3)[q]), found[4 * q + i], table)
+
+    def send_plane(stage, value):
+        p_send[stage] = value
+        for o in offsets:
             pltpu.make_async_remote_copy(
-                src_ref=part.at[stage], dst_ref=recv.at[stage, GROUP - 1 - k], send_sem=g_ss.at[stage],
-                recv_sem=g_rs.at[stage], device_id=peer_of(k), device_id_type=MESH).start()
-
-    def recv_group(stage):
-        pltpu.make_async_copy(recv.at[stage], recv.at[stage], g_rs.at[stage]).wait()
-
-    def sent(stage):
-        pltpu.make_async_copy(recv.at[stage], recv.at[stage], g_ss.at[stage]).wait()
-
-    def relay(stage):
-        recv_group(stage)
-        both = part[stage] + jnp.sum(recv[stage], axis=0)
-        send_group(stage + 1, both[0], both[1], far_peer, far_order)
-
-    def collect(stage, table_out):
-        recv_group(stage)
-        table_out[pl.ds(0, GROUP - 1)] = recv[stage, :, 1]
-        table_out[GROUP - 1] = part[stage, 1]
-        return part[stage, 0] + jnp.sum(recv[stage, :, 0], axis=0)
-
-    send_group(0, vec, table, near_peer, near_order)
+                src_ref=p_send.at[stage], dst_ref=p_recv.at[stage, plane_slot(o)], send_sem=p_ss.at[stage],
+                recv_sem=p_rs.at[stage], device_id=plane_peer(o), device_id_type=MESH).start()
+
+    def settle(buffer, sem):
+        pltpu.make_async_copy(buffer, buffer, sem).wait()
+
+    def plane_sum(stage):
+        settle(p_recv.at[stage], p_rs.at[stage])
+        return p_send[stage] + jnp.sum(p_recv[stage], axis=0)
+
+    def send_depth(src, dst, stage):
+        for k in planes:
+            pltpu.make_async_remote_copy(
+                src_ref=src, dst_ref=dst.at[DEPTH - 1 - k], send_sem=z_ss.at[stage],
+                recv_sem=z_rs.at[stage], device_id=depth_peer(k), device_id_type=MESH).start()
+
+    send_plane(0, table)
 
     for x in (0, T - 1):
         resid_f[pl.ds(T * x, T)] = prepare(flat_of(x, 0), T, 1)
@@ -409,21 +405,28 @@
         def step(i, carry):
             relaxed(src, dst, pl.multiple_of(LO + i * CHUNK, 8), CHUNK)
             return carry
-        lax.fori_loop(0, STEPS, step, 0)
+        lax.fori_loop(0, STEPS, step, 0, unroll=13)
 
     sweep(first_f, e_a_f)
-    relay(0)
     sweep(e_a_f, e_b_f)
-
     def last_sweep(x, carry):
         relaxed(e_b_f, e_c_f, pl.multiple_of((x + 4) * STRIDE, 8), T)
         return carry
 
-    lax.fori_loop(0, T, last_sweep, 0, unroll=4)
+    lax.fori_loop(0, T, last_sweep, 0, unroll=16)
     lc = []
     for s in range(4):
         l_send[s] = line(e_c_f, s, 0)
         lc.append(remote(l_send.at[s], l_recv.at[s], l_ss.at[s], l_rs.at[s], sides[s]))
+
+    table = plane_sum(0)
+    node = table[0:1].astype(jnp.int32)
+    by_row = jnp.where(sub == node // NZ, table[4:5], 0.0)
+    is_lane = (lax.broadcasted_iota(jnp.int32, (NZ, NZ), 0) == lax.rem(node, NZ)).astype(F32)
+    z_send[0] = lax.dot_general(by_row, is_lane, (((1,), (1,)), ((), ())), precision=lax.Precision.HIGHEST,
+                                preferred_element_type=F32)
+    z_send[1] = table
+    send_depth(z_send, z_recv, 0)
 
     def products(bx):
         def add(r, carry):
@@ -436,21 +439,20 @@
             l_out[x] = v
             return al + im, lal + v * im, rl + v * resid_out[x]
         zero = jnp.zeros((T, NZ), F32)
-        return [halves(v) for v in lax.fori_loop(0, BLK, add, (zero, zero, zero), unroll=4)]
+        return [halves(v) for v in lax.fori_loop(0, BLK, add, (zero, zero, zero), unroll=16)]
 
     sums = [products(0), products(1)]
 
-    coarse_resid = collect(1, near_out)
-    coarse_out[1] = coarse_resid
+    settle(z_recv, z_rs.at[0])
+    near_out[pl.ds(0, DEPTH - 1)] = z_recv[:, 1]
+    near_out[DEPTH - 1] = z_send[1]
+    coarse_resid = z_send[0] + jnp.sum(z_recv[:, 0], axis=0)
     loads[4].wait()
     acc = jnp.zeros((4, NZ), F32)
     for k in range(8):
         acc = acc + inverse[:, pl.ds(NZ * k, NZ)] * coarse_resid[k:k + 1]
     acc = jnp.sum(acc, axis=1, keepdims=True)
-    vec = jnp.zeros((8, NZ), F32)
-    base = (gx * n_gy + gy) * 4
-    for i in range(4):
-        vec = vec + jnp.where(node_of == base + i, acc[i:i + 1], 0.0)
+    own_corr = [acc[i:i + 1] for i in range(4)]
 
     for copy in lc:
         copy.wait_recv()
@@ -469,48 +471,55 @@
     for i, (bx, by) in enumerate(blocks):
         for q in range(3):
             table = jnp.where((lane == spot[bx][by]) & (sub == q), found[4 * q + i], table)
-    send_group(2, vec, table, near_peer, near_order)
-    relay(2)
+    for i in range(4):
+        table = jnp.where((lane == 16 * gx + 4 * chip_y + i) & (sub == 3), own_corr[i], table)
+    send_plane(1, table)
     for copy in started:
         copy.wait_send()
-    for stage in range(3):
-        sent(stage)
-    coarse_out[0] = collect(3, far_out)
-    sent(3)
-
-
-def finish(l, image, resid, q, faces, coarse, near, far, guess, pressure, residual, guess_v, press_v, resid_v, load_sem, out_sem):
+    settle(p_recv.at[0], p_ss.at[0])
+    settle(z_recv, z_ss.at[0])
+    t_send[...] = plane_sum(1)
+    send_depth(t_send, t_recv, 1)
+    far_out[DEPTH - 1] = t_send[...]
+    settle(p_recv.at[1], p_ss.at[1])
+    settle(t_recv, z_rs.at[1])
+    far_out[pl.ds(0, DEPTH - 1)] = t_recv[...]
+    settle(t_recv, z_ss.at[1])
+
+
+def finish(l, image, resid, q, faces, near, far, guess, pressure, residual, guess_v, press_v, resid_v, load_sem, out_sem):
     load = pltpu.make_async_copy(guess, guess_v, load_sem)
     load.start()
     gx, gy = lax.axis_index("gx"), lax.axis_index("gy")
-    near_f, far_f = near.reshape(GROUP * 8, NZ), far.reshape(GROUP * 8, NZ)
+    chip_z, chip_y = gy // 4, lax.rem(gy, 4)
+    near_f, far_f = near.reshape(DEPTH * 8, NZ), far.reshape(DEPTH * 8, NZ)
 
     def pick(ref, i):
-        return ref[pl.ds(i, GROUP, stride=8)]
-
-    c = coarse[0]
+        return ref[pl.ds(i, DEPTH, stride=8)]
+
+    c = pick(far_f, 3)
     node = pick(near_f, 0).astype(jnp.int32)
-    at_sub, at_lane = node // NZ, lax.rem(node, NZ)
-    block = jnp.zeros((GROUP, NZ), F32)
-    for s in range(8):
-        line = jnp.broadcast_to(c[s:s + 1], (GROUP, NZ))
+    at_slot = lax.rem(lax.rem(node, NZ) // 16 + 2 * DEPTH - 1 - chip_z, DEPTH)
+    at_lane = node // NZ * 16 + lax.rem(node, 16)
+    block = jnp.zeros((DEPTH, NZ), F32)
+    for s in range(DEPTH):
+        line = jnp.broadcast_to(c[s:s + 1], (DEPTH, NZ))
         hit = jnp.take_along_axis(line, at_lane, axis=1, mode="promise_in_bounds")
-        block = jnp.where(at_sub == s, hit, block)
-    east = pltpu.roll(block, NZ - 4, 1)
-    lane = lax.broadcasted_iota(jnp.int32, (GROUP, NZ), 1)
-    north = jnp.where(lax.rem(lane, 4) == 3, pltpu.roll(pltpu.roll(block, 3, 1), GROUP - 1, 0),
+        block = jnp.where(at_slot == s, hit, block)
+    east = pltpu.roll(block, NZ - 8, 1)
+    lane = lax.broadcasted_iota(jnp.int32, (DEPTH, NZ), 1)
+    north = jnp.where(lax.rem(lane, 8) == 7, pltpu.roll(pltpu.roll(block, 7, 1), DEPTH - 1, 0),
                       pltpu.roll(block, NZ - 1, 1))
     to_east, to_north = block - east, block - north
-    numer = pick(far_f, 2)
+    numer = pick(far_f, 2) + block * pick(near_f, 4)
     denom = (pick(far_f, 1) + 2.0 * block * pick(far_f, 0) + pick(near_f, 1) * block * block
              + pick(near_f, 2) * to_east * to_east + pick(near_f, 3) * to_north * to_north)
 
     def total(v):
         return jnp.sum(jnp.sum(v, axis=0, keepdims=True), axis=1, keepdims=True)
 
-    step = (total(numer) + total(c * coarse[1])) / total(denom)
-    odd = lax.rem(gy, 2)
-    turn = lax.rem(NZ - 8 * gx - 2 * odd, NZ)
+    step = total(numer) / total(denom)
+    turn = lax.rem(NZ - 16 * gx - 2 * chip_y, NZ)
     block, to_east, to_north = (pltpu.roll(v, turn, 1) for v in (block, to_east, to_north))
 
     def value(v, slot, at):
@@ -521,14 +530,14 @@
     def spread(lower, upper):
         return step * jnp.where(high, upper, lower)
 
-    last = GROUP - 1
-    mine = [spread(value(block, last, 4 * bx), value(block, last, 4 * bx + 1)) for bx in range(2)]
-    flux_x = [faces[i] * spread(value(to_east, last, 4 * (i - 1)), value(to_east, last, 4 * (i - 1) + 1))
+    last = DEPTH - 1
+    mine = [spread(value(block, last, 8 * bx), value(block, last, 8 * bx + 1)) for bx in range(2)]
+    flux_x = [faces[i] * spread(value(to_east, last, 8 * (i - 1)), value(to_east, last, 8 * (i - 1) + 1))
               for i in range(3)]
-    below = [jnp.where(odd == 1, value(to_north, last, 4 * bx - 1), value(to_north, last - 1, 4 * bx + 3))
+    below = [jnp.where(chip_y > 0, value(to_north, last, 8 * bx - 1), value(to_north, last - 1, 8 * bx + 7))
              for bx in range(2)]
     flux_y = [faces[3] * spread(*below)] + [
-        faces[3 + i] * spread(value(to_north, last, i - 1), value(to_north, last, 4 + i - 1)) for i in (1, 2)]
+        faces[3 + i] * spread(value(to_north, last, i - 1), value(to_north, last, 8 + i - 1)) for i in (1, 2)]
     flat = resid_v.reshape(T * T, NZ)
     load.wait()
     copies = []
@@ -558,7 +567,7 @@
 
 def body(right_side, guess, conductivity, wet_mask, coarse_map, coarse_inverse):
     tile = jax.ShapeDtypeStruct((T, T, NZ), F32)
-    table = jax.ShapeDtypeStruct((GROUP, 8, NZ), F32)
+    table = jax.ShapeDtypeStruct((DEPTH, 8, NZ), F32)
     hbm = pl.BlockSpec(memory_space=pltpu.HBM)
     vmem = pl.BlockSpec(memory_space=pltpu.VMEM)
     field = pltpu.VMEM((ROWS, STRIDE, NZ), F32)
@@ -566,9 +575,9 @@
     state = pl.pallas_call(
         kernel,
         out_shape=(tile, tile, tile, tile, jax.ShapeDtypeStruct((6, T, NZ), F32),
-                   jax.ShapeDtypeStruct((2, 8, NZ), F32), table, table),
+                   table, table),
         in_specs=[pl.BlockSpec(memory_space=pltpu.SMEM)] + [hbm] * 5,
-        out_specs=(vmem,) * 8,
+        out_specs=(vmem,) * 7,
         scratch_shapes=[
             pltpu.VMEM((3, ROWS, STRIDE, NZ), F32), pltpu.VMEM((T, T, NZ), jnp.int32),
         ] + [field] * 9 + [
@@ -577,9 +586,11 @@
             pltpu.VMEM((4, 6 * T + 8, NZ), F32), pltpu.VMEM((4, 6 * T + 8, NZ), F32),
             pltpu.VMEM((4, 24, NZ), F32), pltpu.VMEM((4, 24, NZ), F32),
             pltpu.VMEM((4, T, NZ), F32), pltpu.VMEM((4, T, NZ), F32),
-            pltpu.VMEM((4, 2, 8, NZ), F32), pltpu.VMEM((4, GROUP - 1, 2, 8, NZ), F32),
+            pltpu.VMEM((2, 8, NZ), F32), pltpu.VMEM((2, PLANE - 1, 8, NZ), F32),
+            pltpu.VMEM((2, 8, NZ), F32), pltpu.VMEM((DEPTH - 1, 2, 8, NZ), F32),
+            pltpu.VMEM((8, NZ), F32), pltpu.VMEM((DEPTH - 1, 8, NZ), F32),
             dma((5,)),
-        ] + [dma((4,))] * 10,
+        ] + [dma((4,))] * 8 + [dma((2,))] * 4,
         compiler_params=pltpu.CompilerParams(
             collective_id=0, has_side_effects=True, vmem_limit_bytes=40 * 1024 * 1024),
     )(*(pltpu.with_memory_space_constraint(array, pltpu.HBM) for array in (
@@ -587,7 +598,7 @@
     return pl.pallas_call(
         finish,
         out_shape=(tile, tile),
-        in_specs=[vmem] * 8 + [hbm],
+        in_specs=[vmem] * 7 + [hbm],
         out_specs=(hbm, hbm),
         scratch_shapes=[pltpu.VMEM((T, T, NZ), F32)] * 3 + [dma, dma((8,))],
         compiler_params=pltpu.CompilerParams(vmem_limit_bytes=16 * 1024 * 1024),

time: 42.3 us -> 38.2 us (0.903)
  Pallas kernels: 41.5 us -> 37.4 us
    pallas_call x1, Pallas kernels: 39.2 us -> 35.2 us  [body(): pl.pallas_call(kernel, out_shape=(tile, tile, tile, tile, jax.ShapeDtypeS...]
where the time goes in v4:
time: 38.2 us; the launch traced here: 38 us
  Pallas kernels  37.4 us (98%)
  between operations  0.64 us (2%)
    pallas_call x1, Pallas kernels, body(): pl.pallas_call(kernel, out_shape=(tile, tile, tile, tile, jax.ShapeDtypeS...  35.2 us
    pallas_call x1, Pallas kernels, body(): pl.pallas_call(finish, out_shape=(tile, tile), in_specs=[vmem] * 7 + [hbm...  2.2 us

profile of v4, /device:TPU:1, one launch (start us, length us, event | category | flops | bytes accessed | tf_op | source)
XLA Modules:
  0.0 38.0 jit_solution(17919192616312135312)
XLA Ops:
  0.6 35.2 %shard_map.77 = (f32[32,32,128]{2,1,0:T(8,128)S(1)}, f32[32,32,128]{2,1,0:T(8,128)S(1)}, f32[32,32,128]{2,1,0:T(8,128)S(1)}, f32[32,32,128]{2,1,0:T(8,128)S(1)},...) custom-call(s32[2,1,2]{2,1,0:T(1,128)} %bitcast.3, f32[4,1024]{1,0:T(4,128)} %cinv.1, ...), custom_call_target="tpu_custom_call" | custom-call | tf_op jit(solution)/shard_map/pallas_call | solution.py:575
  35.8 2.2 %shard_map.78 = (f32[32,32,128]{2,1,0:T(8,128)}, f32[32,32,128]{2,1,0:T(8,128)}) custom-call(f32[32,32,128]{2,1,0:T(8,128)S(1)} %get-tuple-element.9.l, f32[32,32,128]{2,1,0:T(8,128)S(1)} %get-tuple-element.10.image, f32[32,32,128]{2,1,0:T(8,128)S(1)} %get-tuple-element.11.resid, f32[32,32,128]{2,1,0:T(8,128)S(1)} %get-tuple-element.12.q, ...), custom_call_target="tpu_custom_call" | custom-call | tf_op jit(solution)/shard_map/pallas_call | solution.py:598

commit v5 on v4

--- a/solution.py
+++ b/solution.py
@@ -38,7 +38,7 @@
 
 def kernel(
     cmap, cinv, right, guess, conductivity, wet,
-    l_out, image_out, resid_out, q_out, faces_out, near_out, far_out,
+    guess_out, l_out, image_out, resid_out, q_out, faces_out, near_out, far_out,
     ext, mask, w_east, w_north, w_above, diag, dinv, first, e_a, e_b, e_c, inverse,
     a_send, a_recv, b_send, b_recv, k_send, k_recv, l_send, l_recv,
     p_send, p_recv, z_send, z_recv, t_send, t_recv,
@@ -77,28 +77,12 @@
         pltpu.make_async_copy(right, ext.at[(2,) + own], load_sem.at[3]),
         pltpu.make_async_copy(cinv, inverse, load_sem.at[4]),
     ]
-    for copy in loads:
+    for copy in loads[:4]:
         copy.start()
 
     barrier = pltpu.get_barrier_semaphore()
     for peer in [depth_peer(k) for k in planes] + [plane_peer(o) for o in offsets] + corners + list(sides):
         pl.semaphore_signal(barrier, inc=1, device_id=peer, device_id_type=MESH)
-
-    pad = jnp.zeros((8, NZ), F32)
-    wide = jnp.zeros((STRIDE, NZ), F32)
-    for ref in [ext.at[a] for a in range(3)] + [w_east, w_north, w_above, dinv, first]:
-        for r in (0, 1, 2, 3, 36, 37, 38, 39):
-            ref[r] = wide
-        for r in range(4, 36):
-            ref[r, pl.ds(32, 8)] = pad
-    for ref in (e_a, e_b):
-        view(ref)[pl.ds(0, LO)] = jnp.zeros((LO, NZ), F32)
-        view(ref)[pl.ds(LO + CHUNK * STEPS, FLAT - LO - CHUNK * STEPS)] = jnp.zeros(
-            (FLAT - LO - CHUNK * STEPS, NZ), F32)
-    for r in (3, 36):
-        e_c[r] = wide
-    for r in range(4, 36):
-        e_c[r, pl.ds(32, 8)] = pad
 
     sub = lax.broadcasted_iota(jnp.int32, (8, NZ), 0)
     lane = lax.broadcasted_iota(jnp.int32, (8, NZ), 1)
@@ -176,6 +160,23 @@
             k_send[q, pl.ds(18 + 2 * i, 2)] = right_f[pl.ds(flat_of(x2 + i, y2), 2)]
         kc.append(remote(k_send.at[q], k_recv.at[q], k_ss.at[q], k_rs.at[q], corners[q]))
 
+    pad = jnp.zeros((8, NZ), F32)
+    wide = jnp.zeros((STRIDE, NZ), F32)
+    for ref in [ext.at[a] for a in range(3)] + [w_east, w_north, w_above, dinv, first]:
+        for r in (0, 1, 2, 3, 36, 37, 38, 39):
+            ref[r] = wide
+        for r in range(4, 36):
+            ref[r, pl.ds(32, 8)] = pad
+    for ref in (e_a, e_b):
+        view(ref)[pl.ds(0, LO)] = jnp.zeros((LO, NZ), F32)
+        view(ref)[pl.ds(LO + CHUNK * STEPS, FLAT - LO - CHUNK * STEPS)] = jnp.zeros(
+            (FLAT - LO - CHUNK * STEPS, NZ), F32)
+    for r in (3, 36):
+        e_c[r] = wide
+    for r in range(4, 36):
+        e_c[r, pl.ds(32, 8)] = pad
+
+    loads[4].start()
     w_east_f, w_north_f, w_above_f, diag_f, dinv_f, first_f, e_a_f, e_b_f, e_c_f = (
         view(ref) for ref in (w_east, w_north, w_above, diag, dinv, first, e_a, e_b, e_c))
     resid_f, image_f = (ref.reshape(T * T, NZ) for ref in (resid_out, image_out))
@@ -241,37 +242,6 @@
         sums[i][0] -= mid_y[i]
         sums[i][1] += mid_y[i]
 
-    def clear(ref, start, n):
-        ref[pl.ds(start, n)] = jnp.zeros((n, NZ), F32)
-
-    def clear_column(ref, x, y, n):
-        ref[pl.ds(flat_of(x, y), n, stride=STRIDE)] = jnp.zeros((n, NZ), F32)
-
-    for s in range(4):
-        ac[s].wait_recv()
-        for a in range(2):
-            put(fields[a], s, 0, a_recv[s, a])
-
-    @pl.when(gx == 0)
-    def _():
-        clear(cond_f, flat_of(-1, 0), T)
-
-    @pl.when(gx == n_gx - 1)
-    def _():
-        clear(cond_f, flat_of(T, 0), T)
-
-    @pl.when(gy == 0)
-    def _():
-        clear_column(cond_f, 0, -1, T)
-
-    @pl.when(gy == n_gy - 1)
-    def _():
-        clear_column(cond_f, 0, T, T)
-
-    edge_x = [face(row(cond_f, x), row(guess_f, x), row(cond_f, n), row(guess_f, n)) for x, n in ((0, -1), (T - 1, T))]
-    edge_y = [face(column(cond_f, y), column(guess_f, y), column(cond_f, n), column(guess_f, n))
-              for y, n in ((0, -1), (T - 1, T))]
-
     def totals(parts):
         found = []
         for base in range(0, len(parts), 8):
@@ -284,22 +254,34 @@
         return found
 
     blocks = [(bx, by) for bx in range(2) for by in range(2)]
-    w_side = [edge_x[0][1], edge_x[1][1], edge_y[0][1], edge_y[1][1]]
-    for i, w in enumerate((w_side[0], mid_xw, w_side[1], w_side[2], mid_yw, w_side[3])):
-        faces_out[i] = w
-    k_east = [halves(mid_xw), halves(w_side[1])]
-    k_north = [[halves(mid_yw)[bx], halves(w_side[3])[bx]] for bx in range(2)]
-    found = totals(
-        [sums[bx][by] - edge_x[bx][0][by] - edge_y[by][0][bx] for bx, by in blocks]
-        + [k_cell[bx][by] for bx, by in blocks]
-        + [k_east[bx][by] for bx, by in blocks]
-        + [k_north[bx][by] for bx, by in blocks])
+    wx, wy = halves(mid_xw), halves(mid_yw)
+    found = totals([sums[bx][by] for bx, by in blocks] + [k_cell[bx][by] for bx, by in blocks] + wx + wy)
+    here = [lane == spot[bx][by] for bx, by in blocks]
+    cell = [[here[i] & (sub == q) for i in range(4)] for q in range(5)]
     table = jnp.zeros((8, NZ), F32)
-    for i, (bx, by) in enumerate(blocks):
-        here = lane == spot[bx][by]
-        table = jnp.where(here & (sub == 0), packed[i:i + 1], table)
-        for q in range(4):
-            table = jnp.where(here & (sub == (4, 1, 2, 3)[q]), found[4 * q + i], table)
+    for i in range(4):
+        table = jnp.where(cell[0][i], packed[i:i + 1], table)
+        table = jnp.where(cell[1][i], found[4 + i], table)
+        table = jnp.where(cell[4][i], found[i], table)
+    for i in range(2):
+        table = jnp.where(cell[2][i], found[8 + i], table)
+        table = jnp.where(cell[3][2 * i], found[10 + i], table)
+
+    inside = [jnp.where(there, 1.0, 0.0) for there in (gx > 0, gx < n_gx - 1, gy > 0, gy < n_gy - 1)]
+    for copy in ac:
+        copy.wait_recv()
+    beside, out, w_side = [], [], []
+    for s in range(4):
+        cond_line, guess_line = a_recv[s ^ 1, 0] * inside[s], a_recv[s ^ 1, 1]
+        beside.append(cond_line)
+        w_side.append(jnp.minimum(a_send[s, 0], cond_line))
+        out.append(halves(w_side[s] * (a_send[s, 1] - guess_line)))
+    found = totals([out[bx][by] + out[2 + by][bx] for bx, by in blocks] + halves(w_side[1]) + halves(w_side[3]))
+    for i in range(4):
+        table = jnp.where(cell[4][i], table - found[i], table)
+    for i in range(2):
+        table = jnp.where(cell[2][2 + i], found[4 + i], table)
+        table = jnp.where(cell[3][2 * i + 1], found[6 + i], table)
 
     def send_plane(stage, value):
         p_send[stage] = value
@@ -322,6 +304,18 @@
                 recv_sem=z_rs.at[stage], device_id=depth_peer(k), device_id_type=MESH).start()
 
     send_plane(0, table)
+
+    def clear(ref, start, n):
+        ref[pl.ds(start, n)] = jnp.zeros((n, NZ), F32)
+
+    def clear_column(ref, x, y, n):
+        ref[pl.ds(flat_of(x, y), n, stride=STRIDE)] = jnp.zeros((n, NZ), F32)
+
+    for s in range(4):
+        put(cond_f, s, 0, beside[s ^ 1])
+        put(guess_f, s, 0, a_recv[s, 1])
+    for i, w in enumerate((w_side[0], mid_xw, w_side[1], w_side[2], mid_yw, w_side[3])):
+        faces_out[i] = w
 
     for x in (0, T - 1):
         resid_f[pl.ds(T * x, T)] = prepare(flat_of(x, 0), T, 1)
@@ -422,9 +416,14 @@
     table = plane_sum(0)
     node = table[0:1].astype(jnp.int32)
     by_row = jnp.where(sub == node // NZ, table[4:5], 0.0)
-    is_lane = (lax.broadcasted_iota(jnp.int32, (NZ, NZ), 0) == lax.rem(node, NZ)).astype(F32)
-    z_send[0] = lax.dot_general(by_row, is_lane, (((1,), (1,)), ((), ())), precision=lax.Precision.HIGHEST,
-                                preferred_element_type=F32)
+    is_lane = (lax.broadcasted_iota(jnp.int32, (NZ, NZ), 0) == lax.rem(node, NZ)).astype(F32).astype(jnp.bfloat16)
+    pieces = []
+    for _ in range(3):
+        pieces.append(by_row.astype(jnp.bfloat16).astype(F32))
+        by_row = by_row - pieces[-1]
+    by_node = lax.dot_general(jnp.concatenate(pieces).astype(jnp.bfloat16), is_lane, (((1,), (1,)), ((), ())),
+                              preferred_element_type=F32)
+    z_send[0] = by_node[:8] + by_node[8:16] + by_node[16:]
     z_send[1] = table
     send_depth(z_send, z_recv, 0)
 
@@ -437,6 +436,7 @@
             im = diag_f[pl.ds(f, T)] * v - total
             image_out[x] = im
             l_out[x] = v
+            guess_out[x] = guess_f[pl.ds(f, T)]
             return al + im, lal + v * im, rl + v * resid_out[x]
         zero = jnp.zeros((T, NZ), F32)
         return [halves(v) for v in lax.fori_loop(0, BLK, add, (zero, zero, zero), unroll=16)]
@@ -487,9 +487,7 @@
     settle(t_recv, z_ss.at[1])
 
 
-def finish(l, image, resid, q, faces, near, far, guess, pressure, residual, guess_v, press_v, resid_v, load_sem, out_sem):
-    load = pltpu.make_async_copy(guess, guess_v, load_sem)
-    load.start()
+def finish(guess, l, image, resid, q, faces, near, far, pressure, residual, press_v, resid_v, out_sem):
     gx, gy = lax.axis_index("gx"), lax.axis_index("gy")
     chip_z, chip_y = gy // 4, lax.rem(gy, 4)
     near_f, far_f = near.reshape(DEPTH * 8, NZ), far.reshape(DEPTH * 8, NZ)
@@ -539,12 +537,11 @@
     flux_y = [faces[3] * spread(*below)] + [
         faces[3 + i] * spread(value(to_north, last, i - 1), value(to_north, last, 8 + i - 1)) for i in (1, 2)]
     flat = resid_v.reshape(T * T, NZ)
-    load.wait()
     copies = []
     for part in range(4):
         rows = pl.ds(8 * part, 8)
         add = mine[part // 2]
-        press_v[rows] = guess_v[rows] + step * l[rows] + add
+        press_v[rows] = guess[rows] + step * l[rows] + add
         copies.append(pltpu.make_async_copy(press_v.at[rows], pressure.at[rows], out_sem.at[2 * part]))
         copies[-1].start()
         resid_v[rows] = resid[rows] - step * image[rows] - q[rows] * add
@@ -574,10 +571,10 @@
     dma = pltpu.SemaphoreType.DMA
     state = pl.pallas_call(
         kernel,
-        out_shape=(tile, tile, tile, tile, jax.ShapeDtypeStruct((6, T, NZ), F32),
+        out_shape=(tile, tile, tile, tile, tile, jax.ShapeDtypeStruct((6, T, NZ), F32),
                    table, table),
         in_specs=[pl.BlockSpec(memory_space=pltpu.SMEM)] + [hbm] * 5,
-        out_specs=(vmem,) * 7,
+        out_specs=(vmem,) * 8,
         scratch_shapes=[
             pltpu.VMEM((3, ROWS, STRIDE, NZ), F32), pltpu.VMEM((T, T, NZ), jnp.int32),
         ] + [field] * 9 + [
@@ -598,11 +595,11 @@
     return pl.pallas_call(
         finish,
         out_shape=(tile, tile),
-        in_specs=[vmem] * 7 + [hbm],
+        in_specs=[vmem] * 8,
         out_specs=(hbm, hbm),
-        scratch_shapes=[pltpu.VMEM((T, T, NZ), F32)] * 3 + [dma, dma((8,))],
+        scratch_shapes=[pltpu.VMEM((T, T, NZ), F32)] * 2 + [dma((8,))],
         compiler_params=pltpu.CompilerParams(vmem_limit_bytes=16 * 1024 * 1024),
-    )(*state, pltpu.with_memory_space_constraint(guess, pltpu.HBM))
+    )(*state)
 
 
 def solution(mesh):

time: 38.2 us -> 37.5 us (0.982)
  Pallas kernels: 37.4 us -> 36.7 us
    pallas_call x2, Pallas kernels: 37.4 us -> 36.7 us  [the longest x1 35.3 us: body(): pl.pallas_call(kernel, out_shape=(tile, tile, tile, tile, tile, jax.Shape...]
where the time goes in v5:
time: 37.5 us; the launch traced here: 37.4 us
  Pallas kernels  36.7 us (98%)
  between operations  0.64 us (2%)
    pallas_call x1, Pallas kernels, body(): pl.pallas_call(kernel, out_shape=(tile, tile, tile, tile, tile, jax.Shape...  35.3 us
    pallas_call x1, Pallas kernels, body(): pl.pallas_call(finish, out_shape=(tile, tile), in_specs=[vmem] * 8, out_s...  1.47 us

profile of v5, /device:TPU:1, one launch (start us, length us, event | category | flops | bytes accessed | tf_op | source)
XLA Modules:
  0.0 37.4 jit_solution(4909893766078296343)
XLA Ops:
  0.6 35.3 %shard_map.77 = (f32[32,32,128]{2,1,0:T(8,128)S(1)}, f32[32,32,128]{2,1,0:T(8,128)S(1)}, f32[32,32,128]{2,1,0:T(8,128)S(1)}, f32[32,32,128]{2,1,0:T(8,128)S(1)},...) custom-call(s32[2,1,2]{2,1,0:T(1,128)} %bitcast.3, ...), custom_call_target="tpu_custom_call" | custom-call | tf_op jit(solution)/shard_map/pallas_call | solution.py:572
  35.9 1.5 %shard_map.78 = (f32[32,32,128]{2,1,0:T(8,128)}, f32[32,32,128]{2,1,0:T(8,128)}) custom-call(f32[32,32,128]{2,1,0:T(8,128)S(1)} %get-tuple-element.10.guess, f32[32,32,128]{2,1,0:T(8,128)S(1)} %get-tuple-element.11.l, f32[32,32,128]{2,1,0:T(8,128)S(1)} %get-tuple-element.12.image, f32[32,32,128]{2,1,0:T(8,128)S(1)} %get-tuple-element.13.resid, ...), custom_call_target="tpu_custom_call" | custom-call | tf_op jit(solution)/shard_map/pallas_call | solution.py:595

commit v6 on v5

--- a/solution.py
+++ b/solution.py
@@ -38,11 +38,11 @@
 
 def kernel(
     cmap, cinv, right, guess, conductivity, wet,
-    guess_out, l_out, image_out, resid_out, q_out, faces_out, near_out, far_out,
-    ext, mask, w_east, w_north, w_above, diag, dinv, first, e_a, e_b, e_c, inverse,
+    guess_out, l_out, image_out, resid_out, q_out, faces_out, coarse_out, near_out, far_out,
+    ext, mask, w_east, w_north, w_above, diag, dinv, first, e_a, e_b, e_c, inverse, inverse_recv,
     a_send, a_recv, b_send, b_recv, k_send, k_recv, l_send, l_recv,
     p_send, p_recv, z_send, z_recv, t_send, t_recv,
-    load_sem, a_ss, a_rs, b_ss, b_rs, k_ss, k_rs, l_ss, l_rs, p_ss, p_rs, z_ss, z_rs,
+    load_sem, a_ss, a_rs, b_ss, b_rs, k_ss, k_rs, l_ss, l_rs, p_ss, p_rs, z_ss, z_rs, i_ss, i_rs,
 ):
     gx, gy = lax.axis_index("gx"), lax.axis_index("gy")
     n_gx, n_gy = lax.axis_size("gx"), lax.axis_size("gy")
@@ -77,7 +77,7 @@
         pltpu.make_async_copy(right, ext.at[(2,) + own], load_sem.at[3]),
         pltpu.make_async_copy(cinv, inverse, load_sem.at[4]),
     ]
-    for copy in loads[:4]:
+    for copy in loads:
         copy.start()
 
     barrier = pltpu.get_barrier_semaphore()
@@ -176,7 +176,11 @@
     for r in range(4, 36):
         e_c[r, pl.ds(32, 8)] = pad
 
-    loads[4].start()
+    loads[4].wait()
+    for k in planes:
+        pltpu.make_async_remote_copy(
+            src_ref=inverse, dst_ref=inverse_recv.at[DEPTH - 1 - k], send_sem=i_ss.at[0], recv_sem=i_rs.at[0],
+            device_id=depth_peer(k), device_id_type=MESH).start()
     w_east_f, w_north_f, w_above_f, diag_f, dinv_f, first_f, e_a_f, e_b_f, e_c_f = (
         view(ref) for ref in (w_east, w_north, w_above, diag, dinv, first, e_a, e_b, e_c))
     resid_f, image_f = (ref.reshape(T * T, NZ) for ref in (resid_out, image_out))
@@ -380,39 +384,43 @@
         for y in (T, T + 1):
             clear_column(first_f, -2, y, T + 4)
 
-    def around(ref, f, n):
-        at = pl.ds(f, n)
-        v = ref[at]
-        wa = w_above_f[at]
-        total = w_east_f[at] * ref[pl.ds(f + STRIDE, n)]
-        total = total + w_east_f[pl.ds(f - STRIDE, n)] * ref[pl.ds(f - STRIDE, n)]
-        total = total + w_north_f[at] * ref[pl.ds(f + 1, n)]
-        total = total + w_north_f[pl.ds(f - 1, n)] * ref[pl.ds(f - 1, n)]
+    def around(ref, f, n, stride=1):
+        def at(shift=0):
+            return pl.ds(f + shift, n) if stride == 1 else pl.ds(f + shift, n, stride=stride)
+        v = ref[at()]
+        wa = w_above_f[at()]
+        total = w_east_f[at()] * ref[at(STRIDE)]
+        total = total + w_east_f[at(-STRIDE)] * ref[at(-STRIDE)]
+        total = total + w_north_f[at()] * ref[at(1)]
+        total = total + w_north_f[at(-1)] * ref[at(-1)]
         return total + wa * up(v) + down(wa * v), v
 
-    def relaxed(src, dst, f, n):
-        at = pl.ds(f, n)
-        total, v = around(src, f, n)
-        dst[at] = (1.0 - relax) * v + first_f[at] + dinv_f[at] * total
+    def relaxed(src, f, n, stride=1):
+        at = pl.ds(f, n) if stride == 1 else pl.ds(f, n, stride=stride)
+        total, v = around(src, f, n, stride)
+        return (1.0 - relax) * v + first_f[at] + dinv_f[at] * total
 
     def sweep(src, dst):
         def step(i, carry):
-            relaxed(src, dst, pl.multiple_of(LO + i * CHUNK, 8), CHUNK)
+            f = pl.multiple_of(LO + i * CHUNK, 8)
+            dst[pl.ds(f, CHUNK)] = relaxed(src, f, CHUNK)
             return carry
         lax.fori_loop(0, STEPS, step, 0, unroll=13)
 
     sweep(first_f, e_a_f)
     sweep(e_a_f, e_b_f)
+    lc = [None] * 4
+    for s in (2, 3, 0, 1):
+        edge = (T - 1) * (s % 2)
+        l_send[s] = relaxed(e_b_f, flat_of(edge, 0), T) if s < 2 else relaxed(e_b_f, flat_of(0, edge), T, STRIDE)
+        lc[s] = remote(l_send.at[s], l_recv.at[s], l_ss.at[s], l_rs.at[s], sides[s])
+
     def last_sweep(x, carry):
-        relaxed(e_b_f, e_c_f, pl.multiple_of((x + 4) * STRIDE, 8), T)
+        f = pl.multiple_of((x + 4) * STRIDE, 8)
+        e_c_f[pl.ds(f, T)] = relaxed(e_b_f, f, T)
         return carry
 
     lax.fori_loop(0, T, last_sweep, 0, unroll=16)
-    lc = []
-    for s in range(4):
-        l_send[s] = line(e_c_f, s, 0)
-        lc.append(remote(l_send.at[s], l_recv.at[s], l_ss.at[s], l_rs.at[s], sides[s]))
-
     table = plane_sum(0)
     node = table[0:1].astype(jnp.int32)
     by_row = jnp.where(sub == node // NZ, table[4:5], 0.0)
@@ -423,7 +431,17 @@
         by_row = by_row - pieces[-1]
     by_node = lax.dot_general(jnp.concatenate(pieces).astype(jnp.bfloat16), is_lane, (((1,), (1,)), ((), ())),
                               preferred_element_type=F32)
-    z_send[0] = by_node[:8] + by_node[8:16] + by_node[16:]
+    plane_resid = by_node[:8] + by_node[8:16] + by_node[16:]
+    settle(inverse_recv, i_rs.at[0])
+    corr = jnp.zeros((4, NZ), F32)
+    for slot in range(DEPTH):
+        rows = inverse if slot == DEPTH - 1 else inverse_recv.at[slot]
+        acc = rows[:, pl.ds(0, NZ)] * plane_resid[0:1]
+        for k in range(1, 8):
+            acc = acc + rows[:, pl.ds(NZ * k, NZ)] * plane_resid[k:k + 1]
+        place = 8 * (2 * gx + chip_y // 2) + lax.rem(chip_z + 1 + slot, DEPTH)
+        corr = jnp.where(lane[:4] == place, jnp.sum(acc, axis=1, keepdims=True), corr)
+    z_send[0] = jnp.where(sub // 4 == lax.rem(chip_y, 2), jnp.concatenate([corr, corr]), 0.0)
     z_send[1] = table
     send_depth(z_send, z_recv, 0)
 
@@ -443,17 +461,6 @@
 
     sums = [products(0), products(1)]
 
-    settle(z_recv, z_rs.at[0])
-    near_out[pl.ds(0, DEPTH - 1)] = z_recv[:, 1]
-    near_out[DEPTH - 1] = z_send[1]
-    coarse_resid = z_send[0] + jnp.sum(z_recv[:, 0], axis=0)
-    loads[4].wait()
-    acc = jnp.zeros((4, NZ), F32)
-    for k in range(8):
-        acc = acc + inverse[:, pl.ds(NZ * k, NZ)] * coarse_resid[k:k + 1]
-    acc = jnp.sum(acc, axis=1, keepdims=True)
-    own_corr = [acc[i:i + 1] for i in range(4)]
-
     for copy in lc:
         copy.wait_recv()
     for s in range(4):
@@ -471,23 +478,28 @@
     for i, (bx, by) in enumerate(blocks):
         for q in range(3):
             table = jnp.where((lane == spot[bx][by]) & (sub == q), found[4 * q + i], table)
-    for i in range(4):
-        table = jnp.where((lane == 16 * gx + 4 * chip_y + i) & (sub == 3), own_corr[i], table)
     send_plane(1, table)
-    for copy in started:
-        copy.wait_send()
-    settle(p_recv.at[0], p_ss.at[0])
-    settle(z_recv, z_ss.at[0])
+    settle(z_recv, z_rs.at[0])
+    send_plane(2, z_send[0] + jnp.sum(z_recv[:, 0], axis=0))
+    near_out[pl.ds(0, DEPTH - 1)] = z_recv[:, 1]
+    near_out[DEPTH - 1] = z_send[1]
     t_send[...] = plane_sum(1)
     send_depth(t_send, t_recv, 1)
     far_out[DEPTH - 1] = t_send[...]
+    for copy in started:
+        copy.wait_send()
+    settle(inverse_recv, i_ss.at[0])
+    settle(z_recv, z_ss.at[0])
+    settle(p_recv.at[0], p_ss.at[0])
     settle(p_recv.at[1], p_ss.at[1])
+    coarse_out[...] = plane_sum(2)
+    settle(p_recv.at[2], p_ss.at[2])
     settle(t_recv, z_rs.at[1])
     far_out[pl.ds(0, DEPTH - 1)] = t_recv[...]
     settle(t_recv, z_ss.at[1])
 
 
-def finish(guess, l, image, resid, q, faces, near, far, pressure, residual, press_v, resid_v, out_sem):
+def finish(guess, l, image, resid, q, faces, coarse, near, far, pressure, residual, press_v, resid_v, out_sem):
     gx, gy = lax.axis_index("gx"), lax.axis_index("gy")
     chip_z, chip_y = gy // 4, lax.rem(gy, 4)
     near_f, far_f = near.reshape(DEPTH * 8, NZ), far.reshape(DEPTH * 8, NZ)
@@ -495,15 +507,16 @@
     def pick(ref, i):
         return ref[pl.ds(i, DEPTH, stride=8)]
 
-    c = pick(far_f, 3)
+    c = coarse[...]
     node = pick(near_f, 0).astype(jnp.int32)
-    at_slot = lax.rem(lax.rem(node, NZ) // 16 + 2 * DEPTH - 1 - chip_z, DEPTH)
-    at_lane = node // NZ * 16 + lax.rem(node, 16)
+    in_y = lax.rem(node // 4, 4)
+    at_row = lax.rem(node, 4) + 4 * lax.rem(in_y, 2)
+    at_lane = lax.rem(node // 16, 8) + 8 * (2 * (node // NZ) + in_y // 2)
     block = jnp.zeros((DEPTH, NZ), F32)
     for s in range(DEPTH):
         line = jnp.broadcast_to(c[s:s + 1], (DEPTH, NZ))
         hit = jnp.take_along_axis(line, at_lane, axis=1, mode="promise_in_bounds")
-        block = jnp.where(at_slot == s, hit, block)
+        block = jnp.where(at_row == s, hit, block)
     east = pltpu.roll(block, NZ - 8, 1)
     lane = lax.broadcasted_iota(jnp.int32, (DEPTH, NZ), 1)
     north = jnp.where(lax.rem(lane, 8) == 7, pltpu.roll(pltpu.roll(block, 7, 1), DEPTH - 1, 0),
@@ -572,22 +585,22 @@
     state = pl.pallas_call(
         kernel,
         out_shape=(tile, tile, tile, tile, tile, jax.ShapeDtypeStruct((6, T, NZ), F32),
-                   table, table),
+                   jax.ShapeDtypeStruct((8, NZ), F32), table, table),
         in_specs=[pl.BlockSpec(memory_space=pltpu.SMEM)] + [hbm] * 5,
-        out_specs=(vmem,) * 8,
+        out_specs=(vmem,) * 9,
         scratch_shapes=[
             pltpu.VMEM((3, ROWS, STRIDE, NZ), F32), pltpu.VMEM((T, T, NZ), jnp.int32),
         ] + [field] * 9 + [
-            pltpu.VMEM((4, NODES), F32),
+            pltpu.VMEM((4, NODES), F32), pltpu.VMEM((DEPTH - 1, 4, NODES), F32),
             pltpu.VMEM((4, 2, T, NZ), F32), pltpu.VMEM((4, 2, T, NZ), F32),
             pltpu.VMEM((4, 6 * T + 8, NZ), F32), pltpu.VMEM((4, 6 * T + 8, NZ), F32),
             pltpu.VMEM((4, 24, NZ), F32), pltpu.VMEM((4, 24, NZ), F32),
             pltpu.VMEM((4, T, NZ), F32), pltpu.VMEM((4, T, NZ), F32),
-            pltpu.VMEM((2, 8, NZ), F32), pltpu.VMEM((2, PLANE - 1, 8, NZ), F32),
+            pltpu.VMEM((3, 8, NZ), F32), pltpu.VMEM((3, PLANE - 1, 8, NZ), F32),
             pltpu.VMEM((2, 8, NZ), F32), pltpu.VMEM((DEPTH - 1, 2, 8, NZ), F32),
             pltpu.VMEM((8, NZ), F32), pltpu.VMEM((DEPTH - 1, 8, NZ), F32),
             dma((5,)),
-        ] + [dma((4,))] * 8 + [dma((2,))] * 4,
+        ] + [dma((4,))] * 8 + [dma((3,))] * 2 + [dma((2,))] * 2 + [dma((1,))] * 2,
         compiler_params=pltpu.CompilerParams(
             collective_id=0, has_side_effects=True, vmem_limit_bytes=40 * 1024 * 1024),
     )(*(pltpu.with_memory_space_constraint(array, pltpu.HBM) for array in (
@@ -595,7 +608,7 @@
     return pl.pallas_call(
         finish,
         out_shape=(tile, tile),
-        in_specs=[vmem] * 8,
+        in_specs=[vmem] * 9,
         out_specs=(hbm, hbm),
         scratch_shapes=[pltpu.VMEM((T, T, NZ), F32)] * 2 + [dma((8,))],
         compiler_params=pltpu.CompilerParams(vmem_limit_bytes=16 * 1024 * 1024),

time: 37.5 us -> 36.5 us (0.973)
  Pallas kernels: 36.7 us -> 35.8 us
    pallas_call x1, Pallas kernels: 35.3 us -> 34.3 us  [body(): pl.pallas_call(kernel, out_shape=(tile, tile, tile, tile, tile, jax.Shape...]
where the time goes in v6:
time: 36.5 us; the launch traced here: 36.4 us
  Pallas kernels  35.8 us (98%)
  between operations  0.64 us (2%)
    pallas_call x1, Pallas kernels, body(): pl.pallas_call(kernel, out_shape=(tile, tile, tile, tile, tile, jax.Shape...  34.3 us
    pallas_call x1, Pallas kernels, body(): pl.pallas_call(finish, out_shape=(tile, tile), in_specs=[vmem] * 9, out_s...  1.49 us

profile of v6, /device:TPU:1, one launch (start us, length us, event | category | flops | bytes accessed | tf_op | source)
XLA Modules:
  0.0 36.4 jit_solution(3155331443929874322)
XLA Ops:
  0.6 34.3 %shard_map.77 = (f32[32,32,128]{2,1,0:T(8,128)S(1)}, f32[32,32,128]{2,1,0:T(8,128)S(1)}, f32[32,32,128]{2,1,0:T(8,128)S(1)}, f32[32,32,128]{2,1,0:T(8,128)S(1)},...) custom-call(s32[2,1,2]{2,1,0:T(1,128)} %bitcast.3, ...), custom_call_target="tpu_custom_call" | custom-call | tf_op jit(solution)/shard_map/pallas_call | solution.py:585
  34.9 1.5 %shard_map.78 = (f32[32,32,128]{2,1,0:T(8,128)}, f32[32,32,128]{2,1,0:T(8,128)}) custom-call(f32[32,32,128]{2,1,0:T(8,128)S(1)} %get-tuple-element.11.guess, f32[32,32,128]{2,1,0:T(8,128)S(1)} %get-tuple-element.12.l, f32[32,32,128]{2,1,0:T(8,128)S(1)} %get-tuple-element.13.image, f32[32,32,128]{2,1,0:T(8,128)S(1)} %get-tuple-element.14.resid, ...), custom_call_target="tpu_custom_call" | custom-call | tf_op jit(solution)/shard_map/pallas_call | solution.py:608

commit v7 on v6

--- a/solution.py
+++ b/solution.py
@@ -11,7 +11,7 @@
 T = 32
 NZ = 128
 STRIDE = 40
-ROWS = 40
+ROWS = 44
 FLAT = ROWS * STRIDE
 NODES = 1024
 PLANE, DEPTH = 32, 8
@@ -162,25 +162,19 @@
 
     pad = jnp.zeros((8, NZ), F32)
     wide = jnp.zeros((STRIDE, NZ), F32)
-    for ref in [ext.at[a] for a in range(3)] + [w_east, w_north, w_above, dinv, first]:
+    for ref in [ext.at[a] for a in range(3)] + [w_east, w_north, w_above, dinv, first, e_a]:
         for r in (0, 1, 2, 3, 36, 37, 38, 39):
             ref[r] = wide
         for r in range(4, 36):
             ref[r, pl.ds(32, 8)] = pad
-    for ref in (e_a, e_b):
+    for ref in (e_b,):
         view(ref)[pl.ds(0, LO)] = jnp.zeros((LO, NZ), F32)
-        view(ref)[pl.ds(LO + CHUNK * STEPS, FLAT - LO - CHUNK * STEPS)] = jnp.zeros(
-            (FLAT - LO - CHUNK * STEPS, NZ), F32)
+        view(ref)[pl.ds(LO + CHUNK * STEPS, LO)] = jnp.zeros((LO, NZ), F32)
     for r in (3, 36):
         e_c[r] = wide
     for r in range(4, 36):
         e_c[r, pl.ds(32, 8)] = pad
 
-    loads[4].wait()
-    for k in planes:
-        pltpu.make_async_remote_copy(
-            src_ref=inverse, dst_ref=inverse_recv.at[DEPTH - 1 - k], send_sem=i_ss.at[0], recv_sem=i_rs.at[0],
-            device_id=depth_peer(k), device_id_type=MESH).start()
     w_east_f, w_north_f, w_above_f, diag_f, dinv_f, first_f, e_a_f, e_b_f, e_c_f = (
         view(ref) for ref in (w_east, w_north, w_above, diag, dinv, first, e_a, e_b, e_c))
     resid_f, image_f = (ref.reshape(T * T, NZ) for ref in (resid_out, image_out))
@@ -216,6 +210,35 @@
 
     lax.fori_loop(0, T, own_rows, 0, unroll=16)
 
+    def around(ref, f, n, stride=1):
+        def at(shift=0):
+            return pl.ds(f + shift, n) if stride == 1 else pl.ds(f + shift, n, stride=stride)
+        v = ref[at()]
+        wa = w_above_f[at()]
+        total = w_east_f[at()] * ref[at(STRIDE)]
+        total = total + w_east_f[at(-STRIDE)] * ref[at(-STRIDE)]
+        total = total + w_north_f[at()] * ref[at(1)]
+        total = total + w_north_f[at(-1)] * ref[at(-1)]
+        return total + wa * up(v) + down(wa * v), v
+
+    def relaxed(src, f, n, stride=1):
+        at = pl.ds(f, n) if stride == 1 else pl.ds(f, n, stride=stride)
+        total, v = around(src, f, n, stride)
+        return (1.0 - relax) * v + first_f[at] + dinv_f[at] * total
+
+    def own_second(x, carry):
+        f = pl.multiple_of((x + 4) * STRIDE, 8)
+        e_a_f[pl.ds(f, T)] = relaxed(first_f, f, T)
+        return carry
+
+    lax.fori_loop(0, T, own_second, 0, unroll=16)
+
+    loads[4].wait()
+    for k in planes:
+        pltpu.make_async_remote_copy(
+            src_ref=inverse, dst_ref=inverse_recv.at[DEPTH - 1 - k], send_sem=i_ss.at[0], recv_sem=i_rs.at[0],
+            device_id=depth_peer(k), device_id_type=MESH).start()
+
     def cells(bx):
         def add(r, carry):
             acc, kd = carry
@@ -384,22 +407,6 @@
         for y in (T, T + 1):
             clear_column(first_f, -2, y, T + 4)
 
-    def around(ref, f, n, stride=1):
-        def at(shift=0):
-            return pl.ds(f + shift, n) if stride == 1 else pl.ds(f + shift, n, stride=stride)
-        v = ref[at()]
-        wa = w_above_f[at()]
-        total = w_east_f[at()] * ref[at(STRIDE)]
-        total = total + w_east_f[at(-STRIDE)] * ref[at(-STRIDE)]
-        total = total + w_north_f[at()] * ref[at(1)]
-        total = total + w_north_f[at(-1)] * ref[at(-1)]
-        return total + wa * up(v) + down(wa * v), v
-
-    def relaxed(src, f, n, stride=1):
-        at = pl.ds(f, n) if stride == 1 else pl.ds(f, n, stride=stride)
-        total, v = around(src, f, n, stride)
-        return (1.0 - relax) * v + first_f[at] + dinv_f[at] * total
-
     def sweep(src, dst):
         def step(i, carry):
             f = pl.multiple_of(LO + i * CHUNK, 8)
@@ -407,7 +414,11 @@
             return carry
         lax.fori_loop(0, STEPS, step, 0, unroll=13)
 
-    sweep(first_f, e_a_f)
+    for x in (-2, -1, 0, 1, T - 2, T - 1, T, T + 1):
+        e_a_f[pl.ds(flat_of(x, 0), T)] = relaxed(first_f, flat_of(x, 0), T)
+    for y in (-2, -1, 0, 1, T - 2, T - 1, T, T + 1):
+        at = flat_of(-2, y)
+        e_a_f[pl.ds(at, T + 4, stride=STRIDE)] = relaxed(first_f, at, T + 4, STRIDE)
     sweep(e_a_f, e_b_f)
     lc = [None] * 4
     for s in (2, 3, 0, 1):
@@ -421,6 +432,22 @@
         return carry
 
     lax.fori_loop(0, T, last_sweep, 0, unroll=16)
+    def products(bx):
+        def add(r, carry):
+            al, lal, rl = carry
+            x = BLK * bx + r
+            f = pl.multiple_of((x + 4) * STRIDE, 8)
+            total, v = around(e_c_f, f, T)
+            im = diag_f[pl.ds(f, T)] * v - total
+            image_out[x] = im
+            l_out[x] = v
+            guess_out[x] = guess_f[pl.ds(f, T)]
+            return al + im, lal + v * im, rl + v * resid_out[x]
+        zero = jnp.zeros((T, NZ), F32)
+        return [halves(v) for v in lax.fori_loop(0, BLK, add, (zero, zero, zero), unroll=16)]
+
+    sums = [products(0), products(1)]
+
     table = plane_sum(0)
     node = table[0:1].astype(jnp.int32)
     by_row = jnp.where(sub == node // NZ, table[4:5], 0.0)
@@ -445,40 +472,29 @@
     z_send[1] = table
     send_depth(z_send, z_recv, 0)
 
-    def products(bx):
-        def add(r, carry):
-            al, lal, rl = carry
-            x = BLK * bx + r
-            f = pl.multiple_of((x + 4) * STRIDE, 8)
-            total, v = around(e_c_f, f, T)
-            im = diag_f[pl.ds(f, T)] * v - total
-            image_out[x] = im
-            l_out[x] = v
-            guess_out[x] = guess_f[pl.ds(f, T)]
-            return al + im, lal + v * im, rl + v * resid_out[x]
-        zero = jnp.zeros((T, NZ), F32)
-        return [halves(v) for v in lax.fori_loop(0, BLK, add, (zero, zero, zero), unroll=16)]
-
-    sums = [products(0), products(1)]
+    found = totals([sums[bx][q][by] for q in range(3) for bx, by in blocks])
+    table = jnp.zeros((8, NZ), F32)
+    for i in range(4):
+        for q in range(3):
+            table = jnp.where(cell[q][i], found[4 * q + i], table)
 
     for copy in lc:
         copy.wait_recv()
+    losses = [[], []]
+    outs = []
     for s in range(4):
         out = w_side[s] * l_recv[s ^ 1]
-        lost = halves(out), halves(out * l_send[s])
-        for i in range(2):
-            bx, by = (s % 2, i) if s < 2 else (i, s % 2)
-            for q in range(2):
-                sums[bx][q][by] -= lost[q][i]
+        outs.append(out)
+        losses[0].append(halves(out))
+        losses[1].append(halves(out * l_send[s]))
+    lost = totals([losses[q][bx][by] + losses[q][2 + by][bx] for q in range(2) for bx, by in blocks])
+    for i in range(4):
+        for q in range(2):
+            table = jnp.where(cell[q][i], table - lost[4 * q + i], table)
+    send_plane(1, table)
+    for s in range(4):
         at = pl.ds((T - 1) * T * (s % 2), T) if s < 2 else pl.ds((T - 1) * (s % 2), T, stride=T)
-        image_f[at] -= out
-
-    found = totals([sums[bx][q][by] for q in range(3) for bx, by in blocks])
-    table = jnp.zeros((8, NZ), F32)
-    for i, (bx, by) in enumerate(blocks):
-        for q in range(3):
-            table = jnp.where((lane == spot[bx][by]) & (sub == q), found[4 * q + i], table)
-    send_plane(1, table)
+        image_f[at] -= outs[s]
     settle(z_recv, z_rs.at[0])
     send_plane(2, z_send[0] + jnp.sum(z_recv[:, 0], axis=0))
     near_out[pl.ds(0, DEPTH - 1)] = z_recv[:, 1]

time: 36.5 us -> 36.2 us (level)
  Pallas kernels: 35.8 us -> 35.4 us
where the time goes in v7:
time: 36.2 us; the launch traced here: 36.1 us
  Pallas kernels  35.4 us (98%)
  between operations  0.64 us (2%)
    pallas_call x1, Pallas kernels, body(): pl.pallas_call(kernel, out_shape=(tile, tile, tile, tile, tile, jax.Shape...  33.9 us
    pallas_call x1, Pallas kernels, body(): pl.pallas_call(finish, out_shape=(tile, tile), in_specs=[vmem] * 9, out_s...  1.49 us

profile of v7, /device:TPU:1, one launch (start us, length us, event | category | flops | bytes accessed | tf_op | source)
XLA Modules:
  0.0 36.1 jit_solution(10358816123105305446)
XLA Ops:
  0.6 33.9 %shard_map.77 = (f32[32,32,128]{2,1,0:T(8,128)S(1)}, f32[32,32,128]{2,1,0:T(8,128)S(1)}, f32[32,32,128]{2,1,0:T(8,128)S(1)}, f32[32,32,128]{2,1,0:T(8,128)S(1)},...) custom-call(s32[2,1,2]{2,1,0:T(1,128)} %bitcast.3, ...), custom_call_target="tpu_custom_call" | custom-call | tf_op jit(solution)/shard_map/pallas_call | solution.py:601
  34.6 1.5 %shard_map.78 = (f32[32,32,128]{2,1,0:T(8,128)}, f32[32,32,128]{2,1,0:T(8,128)}) custom-call(f32[32,32,128]{2,1,0:T(8,128)S(1)} %get-tuple-element.11.guess, f32[32,32,128]{2,1,0:T(8,128)S(1)} %get-tuple-element.12.l, f32[32,32,128]{2,1,0:T(8,128)S(1)} %get-tuple-element.13.image, f32[32,32,128]{2,1,0:T(8,128)S(1)} %get-tuple-element.14.resid, ...), custom_call_target="tpu_custom_call" | custom-call | tf_op jit(solution)/shard_map/pallas_call | solution.py:624

commit v8 on v7

--- a/solution.py
+++ b/solution.py
@@ -567,24 +567,22 @@
         faces[3 + i] * spread(value(to_north, last, i - 1), value(to_north, last, 8 + i - 1)) for i in (1, 2)]
     flat = resid_v.reshape(T * T, NZ)
     copies = []
-    for part in range(4):
-        rows = pl.ds(8 * part, 8)
-        add = mine[part // 2]
+    for part in range(2):
+        rows = pl.ds(BLK * part, BLK)
+        add = mine[part]
         press_v[rows] = guess[rows] + step * l[rows] + add
         copies.append(pltpu.make_async_copy(press_v.at[rows], pressure.at[rows], out_sem.at[2 * part]))
         copies[-1].start()
         resid_v[rows] = resid[rows] - step * image[rows] - q[rows] * add
         if part == 0:
             resid_v[0] += flux_x[0]
-        elif part == 1:
             resid_v[15] -= flux_x[1]
-        elif part == 2:
+        else:
             resid_v[16] += flux_x[1]
-        else:
             resid_v[31] -= flux_x[2]
-        some = slice(8 * part, 8 * part + 8)
+        some = slice(BLK * part, BLK * part + BLK)
         for y, i, sign in ((0, 0, 1.0), (15, 1, -1.0), (16, 1, 1.0), (31, 2, -1.0)):
-            flat[pl.ds(8 * part * T + y, 8, stride=T)] += sign * flux_y[i][some]
+            flat[pl.ds(BLK * part * T + y, BLK, stride=T)] += sign * flux_y[i][some]
         copies.append(pltpu.make_async_copy(resid_v.at[rows], residual.at[rows], out_sem.at[2 * part + 1]))
         copies[-1].start()
     for copy in copies:

time: 36.2 us -> 36.3 us (level)
  no operation moved by 1% of the time
where the time goes in v8:
time: 36.3 us; the launch traced here: 36.2 us
  Pallas kernels  35.5 us (98%)
  between operations  0.64 us (2%)
    pallas_call x1, Pallas kernels, body(): pl.pallas_call(kernel, out_shape=(tile, tile, tile, tile, tile, jax.Shape...  33.9 us
    pallas_call x1, Pallas kernels, body(): pl.pallas_call(finish, out_shape=(tile, tile), in_specs=[vmem] * 9, out_s...  1.6 us

profile of v8, /device:TPU:1, one launch (start us, length us, event | category | flops | bytes accessed | tf_op | source)
XLA Modules:
  0.0 36.2 jit_solution(7802276564510136070)
XLA Ops:
  0.6 33.9 %shard_map.77 = (f32[32,32,128]{2,1,0:T(8,128)S(1)}, f32[32,32,128]{2,1,0:T(8,128)S(1)}, f32[32,32,128]{2,1,0:T(8,128)S(1)}, f32[32,32,128]{2,1,0:T(8,128)S(1)},...) custom-call(s32[2,1,2]{2,1,0:T(1,128)} %bitcast.3, ...), custom_call_target="tpu_custom_call" | custom-call | tf_op jit(solution)/shard_map/pallas_call | solution.py:599
  34.6 1.6 %shard_map.78 = (f32[32,32,128]{2,1,0:T(8,128)}, f32[32,32,128]{2,1,0:T(8,128)}) custom-call(f32[32,32,128]{2,1,0:T(8,128)S(1)} %get-tuple-element.11.guess, f32[32,32,128]{2,1,0:T(8,128)S(1)} %get-tuple-element.12.l, f32[32,32,128]{2,1,0:T(8,128)S(1)} %get-tuple-element.13.image, f32[32,32,128]{2,1,0:T(8,128)S(1)} %get-tuple-element.14.resid, ...), custom_call_target="tpu_custom_call" | custom-call | tf_op jit(solution)/shard_map/pallas_call | solution.py:622
